TPU v7x, 256 devices: a whole 4x4x8 slice. The times are simulated.
256 devices in a mesh: grp: 4 (over x), pair: 64 (over z, y, core).
Axes of the slice: x: 4, y: 4, z: 8, core: 2. Of those that a mesh axis runs over, the one named last changes fastest.
Arguments:
- blocks: float32 [1024, 128, 128], P(('grp', 'pair')), may hold values from -24 to 24
- block_home: int32 [1024], P(('grp', 'pair')), may hold values from 0 to 1
- block_group: int32 [1024, 1], P(('grp', 'pair')), may hold values from 0 to 3; in each aligned block of 4 rows (0 to 3, 4 to 7, ...) at most 2 rows name the same one
- block_slot: int32 [1024], P(('grp', 'pair')), may hold values from 0 to 1
- pair_funcs: int32 [2, 65536], P(None, ('grp', 'pair')), may hold values from 0 to 1535
- occ_coef: float32 [1536, 16], replicated, may hold values from -0.4 to 0.4
- vir_coef: float32 [1536, 128], replicated, may hold values from -0.4 to 0.4
Outputs:
- half_ints: float32 [65536, 2048], P(('grp', 'pair'))
- orbital_ints: float32 [2048, 2048], P(('grp', 'pair'))
Inputs may be any that keep to these rules, and one draw needn't show every extreme that they name: `block_group`: in the 4 blocks of one device no group is named by more than 2 blocks.
All inputs are finite; a program needn't handle non-finite values.
Results may differ from a plain program's by a relative error of at most 0.0001.
Values sent between devices are 32-bit elements; how exact they have to be, the bound alone decides.
A program may use at most 192 MiB of HBM per device.

v0:
```python
import jax
import jax.numpy as jnp
from jax import lax
from jax.sharding import PartitionSpec as P


def orbital_table(rows_p, rows_q, occ_coef, vir_coef):
    occ_p = jnp.take(occ_coef, rows_p, axis=0)
    occ_q = jnp.take(occ_coef, rows_q, axis=0)
    vir_p = jnp.take(vir_coef, rows_p, axis=0)
    vir_q = jnp.take(vir_coef, rows_q, axis=0)
    table = occ_p[:, :, None] * vir_q[:, None, :] + occ_q[:, :, None] * vir_p[:, None, :]
    return table.reshape(rows_p.shape[0], -1)


def tile_rows(column, tiles, tile, occ_coef, vir_coef):
    offsets = jnp.arange(tile, dtype=jnp.int32)
    picked = (tiles[:, None] * tile + offsets[None, :]).reshape(-1)
    table = orbital_table(
        jnp.take(column[0], picked), jnp.take(column[1], picked), occ_coef, vir_coef
    )
    return table.reshape(tiles.shape[0], tile, -1)


def on_device(blocks, block_home, block_group, block_slot, pair_funcs, occ_coef, vir_coef):
    highest = lax.Precision.HIGHEST
    n_grp = lax.axis_size("grp")
    tile = blocks.shape[1]
    local_tiles = pair_funcs.shape[1] // tile
    capacity = max(2, blocks.shape[0] // 2)
    slots = n_grp * capacity
    column = lax.all_gather(pair_funcs, "grp", axis=1, tiled=True)
    own_table = orbital_table(pair_funcs[0], pair_funcs[1], occ_coef, vir_coef)
    width = own_table.shape[1]
    target = block_group[:, 0]
    partner = target * local_tiles + block_slot
    partner_table = tile_rows(column, partner, tile, occ_coef, vir_coef)
    forward = jnp.einsum(
        "bxy,byc->bxc", blocks, partner_table, precision=highest, preferred_element_type=jnp.float32
    )
    home_hot = (block_home[None, :] == jnp.arange(local_tiles, dtype=jnp.int32)[:, None]).astype(
        jnp.float32
    )
    half_forward = jnp.einsum(
        "sb,bxc->sxc", home_hot, forward, precision=highest, preferred_element_type=jnp.float32
    )
    group_hot = (target[:, None] == jnp.arange(n_grp, dtype=jnp.int32)[None, :]).astype(jnp.int32)
    rank = jnp.sum((jnp.cumsum(group_hot, axis=0) - group_hot) * group_hot, axis=1)
    place = target * capacity + rank
    place_hot = (jnp.arange(slots, dtype=jnp.int32)[:, None] == place[None, :]).astype(jnp.float32)
    outgoing = jnp.einsum(
        "jb,bxy->jxy", place_hot, blocks, precision=highest, preferred_element_type=jnp.float32
    )
    code = (block_home + local_tiles * block_slot).astype(jnp.float32)
    sent_code = jnp.dot(place_hot, code, precision=highest, preferred_element_type=jnp.float32)
    arrived, arrived_code = (
        lax.all_to_all(outgoing, "grp", split_axis=0, concat_axis=0, tiled=True),
        lax.all_to_all(sent_code, "grp", split_axis=0, concat_axis=0, tiled=True),
    )
    arrived_code = arrived_code.astype(jnp.int32)
    source_group = jnp.arange(slots, dtype=jnp.int32) // capacity
    source_tile = source_group * local_tiles + arrived_code % local_tiles
    my_slot = arrived_code // local_tiles
    source_table = tile_rows(column, source_tile, tile, occ_coef, vir_coef)
    mirrored = jnp.einsum(
        "byx,byc->bxc", arrived, source_table, precision=highest, preferred_element_type=jnp.float32
    )
    slot_hot = (my_slot[None, :] == jnp.arange(local_tiles, dtype=jnp.int32)[:, None]).astype(
        jnp.float32
    )
    half_mirror = jnp.einsum(
        "sb,bxc->sxc", slot_hot, mirrored, precision=highest, preferred_element_type=jnp.float32
    )
    half = (half_forward + half_mirror).reshape(local_tiles * tile, width)
    contract = (((0,), (0,)), ((), ()))
    partial_value = lax.dot_general(
        half, own_table, contract, precision=highest, preferred_element_type=jnp.float32
    )
    summed = lax.psum_scatter(partial_value, ("grp", "pair"), scatter_dimension=0, tiled=True)
    return (half, summed)


def solution(mesh):
    placed = (
        P(("grp", "pair"), None, None),
        P(("grp", "pair")),
        P(("grp", "pair"), None),
        P(("grp", "pair")),
        P(None, ("grp", "pair")),
        P(),
        P(),
    )
    return jax.shard_map(
        on_device,
        mesh=mesh,
        in_specs=placed,
        out_specs=(P(("grp", "pair"), None), P(("grp", "pair"), None)),
        check_vma=False,
    )
```

profile of v0, /device:TPU:8, one launch (start us, length us, event | category | flops | bytes accessed | tf_op | source)
XLA Modules:
  0.0 1458.4 jit_solution(4999105053269272981)
XLA Ops:
  7.2 0.0 copy-start
  7.2 0.8 fusion.13
  8.0 0.8 select_reduce_fusion
  8.9 0.7 add_multiply_fusion
  9.5 0.9 convolution_bitcast_fusion.1
  10.4 0.7 all_to_all.9
  11.1 4.3 all-to-all-start
  15.4 11.7 all_gather.3
  27.1 1.2 copy.61
  28.2 0.1 compare_select_fusion.5
  28.3 2.3 gather_fusion
  30.6 2.3 gather_fusion.2
  32.9 0.1 compare_and_fusion.4
  33.0 0.0 copy-start.6
  33.0 1.0 gather_fusion.1
  34.1 1.0 gather_fusion.4
  35.1 0.0 copy-start.5
  35.1 1.0 gather_fusion.3
  36.2 1.0 gather_fusion.5
  37.3 0.7 gather_fusion.14
  38.0 0.7 gather_fusion.13
  38.8 0.7 gather_fusion.12
  39.5 0.7 gather_fusion.15
  40.2 0.6 fusion.5
  40.9 0.9 copy.67
  41.7 0.2 broadcast_select_fusion.6
  42.0 0.2 broadcast_select_fusion.4
  42.2 5.4 multiply_add_fusion.1
  47.6 4.9 add.160
  52.5 9.8 convolution_bitcast_fusion
  62.3 5.5 copy.64
  67.8 0.1 broadcast_select_fusion.10
  68.0 0.1 broadcast_select_fusion.8
  68.1 3.1 multiply_add_fusion.2
  71.2 0.0 all-to-all-done
  71.2 3.5 all-to-all-start.1
  74.7 0.2 reduce-scatter.2.cloned.1.call-start
  75.0 0.1 convert_element_type.26
  75.1 0.1 fusion.7
  75.1 4.5 gather_fusion.6
  79.7 4.5 gather_fusion.8
  84.2 0.1 fusion.12
  84.3 0.1 compare_and_fusion
  84.4 2.8 gather_fusion.10
  87.2 2.8 gather_fusion.9
  90.0 4.0 gather_fusion.7
  94.0 2.8 gather_fusion.11
  96.8 1.4 broadcast_select_fusion.2
  98.2 0.3 broadcast_select_fusion
  98.6 9.5 multiply_add_fusion
  108.0 9.3 add.170
  117.3 0.0 all-to-all-done.1
  117.3 10.3 fusion.35
  127.6 0.0 copy-start.7
  127.6 7.9 fusion
  135.6 4.9 convolution_add_fusion
  140.5 0.0 copy-start.4
  140.5 1.2 copy.72
  141.7 0.0 copy-start.3
  141.7 0.3 copy-done.4
  142.1 17.4 %fusion.2 = f32[2048,2048]{1,0:T(8,128)} fusion(f32[256,2048]{1,0:T(8,128)S(1)} %bitcast.69, f32[32,8,16,128]{3,2,1,0:T(8,128)S(1)} %bitcast.71), kind=kOutput, calls=%fused_computation.22 | convolution fusion | flops 12884901888 | bytes 20971520 | tf_op jit(solution)/shard_map/dot_general | solution.py:76
  159.5 0.0 reduce-scatter.2.cloned.1.call-update
  159.5 0.0 copy-start.1
  159.5 1292.0 %reduce-scatter.2.cloned.1.call-done = f32[8,2048]{1,0:T(8,128)} async-done(((f32[2048,2048]{1,0:T(8,128)}), f32[8,2048]{1,0:T(8,128)}) %reduce-scatter.2.cloned.1.call-update) | async-done | bytes 65552 | tf_op jit(solution)/shard_map/reduce_scatter | solution.py:79
  (22 shorter events, 0.2 us)
Async XLA Ops:
  7.2 27.9 %copy-start = (f32[1536,128]{1,0:T(8,128)S(1)}, f32[1536,128]{1,0:T(8,128)}, u32[]{:S(2)}) copy-start(f32[1536,128]{1,0:T(8,128)} %param.29) | copy-start | bytes 2359300
  11.1 60.2 %all-to-all-start = ((f32[4,2,1]{1,2,0:T(1,128)}), f32[4,2,1]{1,2,0:T(1,128)S(1)}, u32[]{:S(2)}, u32[]{:S(2)}) async-start(f32[4,2,1]{1,2,0:T(1,128)} %bitcast.8), calls=%async_computation | async-start | bytes 4096 | tf_op jit(solution)/shard_map/all_to_all | solution.py:58
  33.0 4.2 copy-start.6
  35.1 5.1 copy-start.5
  71.2 46.1 %all-to-all-start.1 = ((f32[8,128,128]{2,1,0:T(8,128)}), f32[8,128,128]{2,1,0:T(8,128)S(1)}, u32[]{:S(2)}, u32[]{:S(2)}) async-start(f32[8,128,128]{2,1,0:T(8,128)} %copy.67), calls=%async_computation.1 | async-start | bytes 1048576 | tf_op jit(solution)/shard_map/all_to_all | solution.py:57
  74.7 1376.8 %reduce-scatter.2.cloned.1.call-start = ((), (), s32[]{:S(2)}) async-start(), calls=%async_computation.3 | async-start | bytes 16842752 | tf_op jit(solution)/shard_map/reduce_scatter | solution.py:79
  127.6 8.0 copy-start.2
  127.6 8.0 copy-start.7
  140.5 1.6 copy-start.4
  141.7 17.7 %copy-start.3 = (f32[2,128,2048]{2,1,0:T(8,128)}, f32[2,128,2048]{2,1,0:T(8,128)S(1)}, u32[]{:S(2)}) copy-start(f32[2,128,2048]{2,1,0:T(8,128)S(1)} %copy.72) | copy-start | bytes 6291460
  159.5 1292.0 %copy-start.1 = (f32[1536,128]{1,0:T(8,128)S(1)}, f32[1536,128]{1,0:T(8,128)}, u32[]{:S(2)}) copy-start(f32[1536,128]{1,0:T(8,128)} %param.29) | copy-start | bytes 2359300
Sparse Core Ops, SparseCore 0:
  159.6 1291.8 reduce-scatter.1
where the time goes:
time: 1460 us
  waiting for transfers between devices  1290 us (88%)
  local copies, waits for them, and re-layouts  57.2 us (4%)
  matrix products  51.8 us (4%)
  other arithmetic  23.3 us (2%)
    reduce_scatter x1, waiting for transfers between devices, on_device(): lax.psum_scatter(partial_value, ('grp', 'pair'), scatter_dimension=0, til...  1290 us
  transfers between devices with their start and end apart: 3, of which 1 were waited for; matrix products, arithmetic and copies ran while one was open for 6% of the time, Pallas kernels for 0%

commit v1 on v0

v1 whole, which is shorter than its diff:
```python
import functools

import jax
import jax.numpy as jnp
from jax import lax
from jax.experimental import pallas as pl
from jax.experimental.pallas import tpu as pltpu
from jax.sharding import PartitionSpec as P

F32, BF16 = jnp.float32, jnp.bfloat16


def split(value):
    high = value.astype(BF16)
    return high, (value - high.astype(F32)).astype(BF16)


def dot(lhs, rhs, contract):
    return lax.dot_general(lhs, rhs, (contract, ((), ())), preferred_element_type=F32)


NN, NT = ((1,), (0,)), ((1,), (1,))


def dot3(lh, ll, rh, rl, contract):
    return dot(lh, rh, contract) + (dot(lh, rl, contract) + dot(ll, rh, contract))


def pack_coef(occ_ref, vir_ref, coef_ref):
    n_occ, n_vir = occ_ref.shape[1], vir_ref.shape[1]
    width = n_vir + n_occ
    coef_ref[:n_vir], coef_ref[width : width + n_vir] = split(vir_ref[...].T)
    coef_ref[n_vir:width], coef_ref[width + n_vir :] = split(occ_ref[...].T)


def gather_table(coef_ref, funcs_ref, tab_h, tab_l, n_occ, n_vir, step):
    nb = coef_ref.shape[1]
    width = n_vir + n_occ
    rows = funcs_ref.shape[1]

    def body(c, carry):
        cols = pl.ds(pl.multiple_of(c * step, step), step)
        got = []
        for f in range(2):
            func = funcs_ref[f : f + 1, cols]
            hot = lax.broadcasted_iota(jnp.int32, (nb, step), 0) == func
            hot = jnp.where(hot, 1.0, 0.0).astype(BF16)
            both = dot(coef_ref[...], hot, NN)
            got.append(both[:width] + both[width:])
        (vir_p, occ_p), (vir_q, occ_q) = [(g[:n_vir], g[n_vir:]) for g in got]
        for i in range(n_occ):
            entry = occ_p[i : i + 1] * vir_q + occ_q[i : i + 1] * vir_p
            high, low = split(entry)
            tab_h[i * n_vir : (i + 1) * n_vir, cols] = high
            tab_l[i * n_vir : (i + 1) * n_vir, cols] = low
        return carry

    lax.fori_loop(0, rows // step, body, 0)


def build_matrix(home_ref, part_ref, blocks_ref, flip, mat_h, mat_l, tiles_dev):
    count, tile, _ = blocks_ref.shape
    n_tiles = mat_h.shape[0] // tile
    per_dev = count * tiles_dev // n_tiles
    for b in range(count):
        flip[b] = blocks_ref[b].T

    def body(step, carry):
        h, t = step // n_tiles, lax.rem(step, n_tiles)
        dev_h, dev_t = h // tiles_dev, t // tiles_dev
        total = jnp.zeros((tile, tile), F32)
        for j in range(per_dev):
            b = dev_h * per_dev + j
            here = jnp.logical_and(home_ref[b] == h, part_ref[b] == t)
            total = total + jnp.where(here, blocks_ref[b], 0.0)
            b = dev_t * per_dev + j
            here = jnp.logical_and(home_ref[b] == t, part_ref[b] == h)
            total = total + jnp.where(here, flip[b], 0.0)
        high, low = split(total)
        rows = pl.ds(pl.multiple_of(h * tile, tile), tile)
        cols = pl.ds(pl.multiple_of(t * tile, tile), tile)
        mat_h[rows, cols] = high
        mat_l[rows, cols] = low
        return carry

    lax.fori_loop(0, n_tiles * n_tiles, body, 0)


def column_kernel(n_occ, n_vir, tiles_dev, home_ref, part_ref, funcs_ref, occ_ref, vir_ref, blocks_ref, half_ref, part_out,
                  coef_ref, tab_h, tab_l, mat_h, mat_l, flip, g_h, g_l):
    grp = lax.axis_index("grp")
    width, rows = tab_h.shape
    mine = part_out.shape[0]
    own = half_ref.shape[0]
    pack_coef(occ_ref, vir_ref, coef_ref)
    gather_table(coef_ref, funcs_ref, tab_h, tab_l, n_occ, n_vir, 256)
    build_matrix(home_ref, part_ref, blocks_ref, flip, mat_h, mat_l, tiles_dev)
    share = pl.ds(pl.multiple_of(grp * mine, mine), mine)

    def make_g(c, carry):
        cols = pl.ds(pl.multiple_of(c * 256, 256), 256)
        g = dot3(tab_h[share, :], tab_l[share, :], mat_h[:, cols], mat_l[:, cols], NN)
        g_h[:, cols], g_l[:, cols] = split(g)
        return carry

    lax.fori_loop(0, rows // 256, make_g, 0)
    local = pl.ds(pl.multiple_of(grp * own, own), own)

    def outputs(c, carry):
        cols = pl.ds(pl.multiple_of(c * 256, 256), 256)
        part_out[:, cols] = dot3(g_h[...], g_l[...], tab_h[cols, :], tab_l[cols, :], NT)
        half_ref[:, cols] = dot3(mat_h[local, :], mat_l[local, :], tab_h[cols, :], tab_l[cols, :], NT)
        return carry

    lax.fori_loop(0, width // 256, outputs, 0)


def on_device(blocks, block_home, block_group, block_slot, pair_funcs, occ_coef, vir_coef):
    n_grp = lax.axis_size("grp")
    grp = lax.axis_index("grp")
    tile = blocks.shape[1]
    own = pair_funcs.shape[1]
    tiles_dev = own // tile
    n_occ, n_vir = occ_coef.shape[1], vir_coef.shape[1]
    width = n_occ * n_vir
    rows = own * n_grp
    count = blocks.shape[0] * n_grp
    mine = width // n_grp
    home = grp * tiles_dev + block_home
    part = block_group[:, 0] * tiles_dev + block_slot
    funcs = lax.all_gather(pair_funcs, "grp", axis=1, tiled=True)
    codes = lax.all_gather(jnp.stack([home, part]), "grp", axis=1, tiled=True)
    every = lax.all_gather(blocks, "grp", axis=0, tiled=True)
    vmem = pl.BlockSpec(memory_space=pltpu.VMEM)
    smem = pl.BlockSpec(memory_space=pltpu.SMEM)
    half, partial = pl.pallas_call(
        functools.partial(column_kernel, n_occ, n_vir, tiles_dev),
        out_shape=(jax.ShapeDtypeStruct((own, width), F32), jax.ShapeDtypeStruct((mine, width), F32)),
        in_specs=[smem, smem, vmem, vmem, vmem, vmem],
        out_specs=(vmem, vmem),
        scratch_shapes=[
            pltpu.VMEM((2 * (n_occ + n_vir), occ_coef.shape[0]), BF16),
            pltpu.VMEM((width, rows), BF16),
            pltpu.VMEM((width, rows), BF16),
            pltpu.VMEM((rows, rows), BF16),
            pltpu.VMEM((rows, rows), BF16),
            pltpu.VMEM((count, tile, tile), F32),
            pltpu.VMEM((mine, rows), BF16),
            pltpu.VMEM((mine, rows), BF16),
        ],
        compiler_params=pltpu.CompilerParams(vmem_limit_bytes=56 * 2**20),
    )(codes[0], codes[1], funcs, occ_coef, vir_coef, every)
    return half, lax.psum_scatter(partial, "pair", scatter_dimension=0, tiled=True)


def solution(mesh):
    both = ("grp", "pair")
    placed = (P(both, None, None), P(both), P(both, None), P(both), P(None, both), P(), P())
    return jax.shard_map(
        on_device,
        mesh=mesh,
        in_specs=placed,
        out_specs=(P(both, None), P(both, None)),
        check_vma=False,
    )
```

time: 1460 us -> 275 us (0.19)
  waiting for transfers between devices: 1290 us -> 203 us
  local copies, waits for them, and re-layouts: 57.2 us -> 4.75 us
  matrix products: 51.8 us -> 0 us
  Pallas kernels: 0 us -> 30.5 us
  other arithmetic: 23.3 us -> 0.7 us
    reduce_scatter x1 -> x0, waiting for transfers between devices: 1290 us -> none  [on_device(): lax.psum_scatter(partial_value, ('grp', 'pair'), scatter_dimension=0, til...]
    unnamed x1 -> x3, waiting for transfers between devices: 0.02 us -> 196 us
    dot_general x7 -> x0, matrix products: 51.8 us -> none  [the longest x1 17.4 us: on_device(): lax.dot_general(half, own_table, contract, precision=highest, preferred_e...]
    gather x16 -> x0, local copies, waits for them, and re-layouts: 33.1 us -> none  [the longest x2 6.82 us: tile_rows(): jnp.take(column[1], picked)]
    pallas_call x0 -> x1, Pallas kernels: none -> 30.5 us  [on_device(): pl.pallas_call(functools.partial(column_kernel, n_occ, n_vir, tiles_dev),...]
    add x3 -> x0, other arithmetic: 18 us -> none  [orbital_table(): occ_p[:, :, None] * vir_q[:, None, :]]
    add x3 -> x0, local copies, waits for them, and re-layouts: 15.4 us -> none  [the longest x2 14.2 us: orbital_table(): occ_p[:, :, None] * vir_q[:, None, :]]
  transfers between devices with their start and end apart: 3 -> 2, of which waited for: 1 -> 2; matrix products, arithmetic and copies ran while one was open for 6% -> 1% of each run, Pallas kernels for 0% -> 0%
where the time goes in v1:
time: 275 us; the launch traced here: 274 us
  waiting for transfers between devices  203 us (74%)
  Pallas kernels  30.5 us (11%)
  blocking collectives  20.6 us (7%)
  between operations  14.7 us (5%)
  local copies, waits for them, and re-layouts  4.75 us (2%)
    unnamed x3, waiting for transfers between devices  196 us
    pallas_call x1, Pallas kernels, on_device(): pl.pallas_call(functools.partial(column_kernel, n_occ, n_vir, tiles_dev),...  30.5 us
    all_gather x1, blocking collectives, on_device(): funcs = lax.all_gather(pair_funcs, 'grp', axis=1, tiled=True)  10.9 us
    all_gather x1, blocking collectives, on_device(): codes = lax.all_gather(jnp.stack([home, part]), 'grp', axis=1, tiled=True)  9.72 us
    all_gather x1, waiting for transfers between devices, on_device(): every = lax.all_gather(blocks, 'grp', axis=0, tiled=True)  7.23 us
  transfers between devices with their start and end apart: 2, of which 2 were waited for; matrix products, arithmetic and copies ran while one was open for 1% of the time, Pallas kernels for 0%

profile of v1, /device:TPU:8, one launch (start us, length us, event | category | flops | bytes accessed | tf_op | source)
XLA Modules:
  0.0 274.5 jit_solution(3673147696316917887)
XLA Ops:
  7.2 0.0 copy-start
  7.2 0.0 all-gather.3.cloned.1.call-start
  7.2 0.7 all-gather.3.cloned.1.call-update
  7.9 0.0 all-reduce.3.cloned.1.call-start
  8.0 0.7 fusion
  8.7 9.7 %all-gather = s32[4,4,2]{1,2,0:T(2,128)S(1)} all-gather(s32[1,4,2]{1,2,0:T(2,128)S(1)} %add_bitcast_fusion), channel_id=1, replica_groups=mesh['grp'=4,'pair'=64] {'grp'}, dimensions={0}, use_global_device_ids=true | all-gather | bytes 160 | tf_op jit(solution)/shard_map/all_gather | solution.py:132
  18.4 0.1 reshape.7
  18.5 2.1 copy.12.occ_ref
  20.6 10.9 %all_gather.10.funcs_ref = s32[2,1024]{1,0:T(2,128)} all-gather(s32[2,256]{1,0:T(2,128)} %param.11), channel_id=1, replica_groups=mesh['grp'=4,'pair'=64] {'grp'}, dimensions={1}, use_global_device_ids=true | all-gather | bytes 10240 | tf_op jit(solution)/shard_map/all_gather | solution.py:131
  31.5 0.5 slice_bitcast_fusion
  32.0 7.2 %all-gather.3.cloned.1.call-done.blocks_ref = f32[16,128,128]{2,1,0:T(8,128)} async-done(((f32[4,128,128]{2,1,0:T(8,128)}), f32[16,128,128]{2,1,0:T(8,128)}) %all-gather.3.cloned.1.call-update) | async-done | bytes 1048592 | tf_op jit(solution)/shard_map/all_gather | solution.py:133
  39.2 30.5 %shard_map.86 = (f32[256,2048]{1,0:T(8,128)}, f32[512,2048]{1,0:T(8,128)}) custom-call(s32[16]{0:T(128)} %get-tuple-element.7.home_ref, s32[16]{0:T(128)} %get-tuple-element.6.part_ref, s32[2,1024]{1,0:T(2,128)} %all_gather.10.funcs_ref, f32[1536,16]{1,0:T(8,128)} %copy.12.occ_ref, f32[1536,128]{1,0:T(8,128)} %vir_ref.1, ...), custom_call_target="tpu_custom_call" | custom-call | tf_op jit(solution)/shard_map/pallas_call | solution.py:136
  69.8 0.0 all-reduce.3.cloned.1.call-update
  69.8 0.0 copy-done
  69.8 0.6 dynamic-slice
  71.0 195.1 %all-reduce.3.cloned.1.call-done = f32[512,2048]{1,0:T(8,128)} async-done(((f32[512,2048]{1,0:T(8,128)}), f32[512,2048]{1,0:T(8,128)}) %all-reduce.3.cloned.1.call-update) | async-done | bytes 4194320
  266.2 1.5 constant_dynamic-slice_fusion
  (2 shorter events, 0.0 us)
Async XLA Ops:
  7.2 62.6 %copy-start = (u32[256]{0:T(256)S(1)}, u32[256]{0:T(256)}, u32[]{:S(2)}) copy-start(u32[256]{0:T(256)} %constant.15) | copy-start | bytes 3076
  7.2 32.1 %all-gather.3.cloned.1.call-start = ((), (), s32[]{:S(2)}) async-start(), calls=%async_computation | async-start | bytes 1310720 | tf_op jit(solution)/shard_map/all_gather | solution.py:133
  7.9 258.2 %all-reduce.3.cloned.1.call-start = ((), (), s32[]{:S(2)}) async-start(), calls=%async_computation.1 | async-start | bytes 8388608
Sparse Core Ops, SparseCore 0:
  9.8 29.3 all-gather.2
  69.9 196.2 all-reduce.2

commit v2 on v1

v2 whole, which is shorter than its diff:
```python
import functools

import jax
import jax.numpy as jnp
from jax import lax
from jax.experimental import pallas as pl
from jax.experimental.pallas import tpu as pltpu
from jax.sharding import PartitionSpec as P

F32, BF16, I32 = jnp.float32, jnp.bfloat16, jnp.int32
NZ, NY, NC = 8, 4, 2
STEP = 256
SUB = 8
INFO = 8
MESH = pl.DeviceIdType.MESH
NN, NT = ((1,), (0,)), ((1,), (1,))


def split(value):
    high = value.astype(BF16)
    return high, (value - high.astype(F32)).astype(BF16)


def dot(lhs, rhs, contract):
    return lax.dot_general(lhs, rhs, (contract, ((), ())), preferred_element_type=F32)


def dot3(lh, ll, rh, rl, contract):
    return dot(lh, rh, contract) + (dot(lh, rl, contract) + dot(ll, rh, contract))


def chunk(c, step=STEP):
    return pl.ds(pl.multiple_of(c * step, step), step)


def ring(i, n):
    return lax.rem(i + 2 * n, n)


class Chain:
    def __init__(self, me, size, sign, length, piece, landing, send_sem, recv_sem, to):
        self.me, self.size, self.sign, self.length = me, size, sign, length
        self.piece, self.landing, self.send_sem, self.recv_sem, self.to = piece, landing, send_sem, recv_sem, to

    def owner(self, j):
        return ring(self.me + self.sign * (self.length - j), self.size)

    def copy(self, j):
        return pltpu.make_async_remote_copy(
            src_ref=self.piece(self.owner(j)),
            dst_ref=self.landing.at[j],
            send_sem=self.send_sem.at[j],
            recv_sem=self.recv_sem.at[j],
            device_id=self.to(ring(self.me + self.sign, self.size)),
            device_id_type=MESH,
        )

    def start(self):
        if self.length:
            self.copy(0).start()

    def advance(self, j):
        if j < self.length - 1:
            self.copy(j).wait_recv()
            here = self.piece(self.owner(j + 1))
            here[...] = here[...] + self.landing[j]
            self.copy(j + 1).start()

    def arrive(self, total):
        if not self.length:
            return total
        self.copy(self.length - 1).wait_recv()
        return total + self.landing[self.length - 1]

    def drain(self):
        for j in range(self.length):
            self.copy(j).wait_send()


def lengths(n):
    far, near = n // 2, n - 1 - n // 2
    return ((far, near), (near, far))


def pack_coef(occ_ref, vir_ref, coef_ref):
    n_occ, n_vir = occ_ref.shape[0], vir_ref.shape[1]
    width = n_vir + n_occ
    coef_ref[:n_vir], coef_ref[width : width + n_vir] = split(vir_ref[...].T)
    coef_ref[n_vir:width], coef_ref[width + n_vir :] = split(occ_ref[...])


def table_part(info_ref, g, first, coef_ref, tab_h, tab_l, n_occ, n_vir):
    nb = coef_ref.shape[1]
    width = n_vir + n_occ
    got = []
    for f in range(2):
        func = info_ref[g, first + f : first + f + 1, :]
        hot = lax.broadcasted_iota(I32, (nb, STEP), 0) == func
        hot = jnp.where(hot, 1.0, 0.0).astype(BF16)
        both = dot(coef_ref[...], hot, NN)
        got.append(both[:width] + both[width:])
    (vir_p, occ_p), (vir_q, occ_q) = [(v[:n_vir], v[n_vir:]) for v in got]
    cols = chunk(g)
    for i in range(n_occ):
        entry = occ_p[i : i + 1] * vir_q + occ_q[i : i + 1] * vir_p
        high, low = split(entry)
        tab_h[i * n_vir : (i + 1) * n_vir, cols] = high
        tab_l[i * n_vir : (i + 1) * n_vir, cols] = low


def build_matrix(info_ref, every, flip, mat_h, mat_l, tiles_dev):
    n_grp, per_dev, tile, _ = every.shape
    n_tiles = n_grp * tiles_dev
    for g in range(n_grp):
        for j in range(per_dev):
            flip[g, j] = every[g, j].T

    def body(step, carry):
        h, t = lax.div(step, n_tiles), lax.rem(step, n_tiles)
        dev_h, dev_t = lax.div(h, tiles_dev), lax.div(t, tiles_dev)
        total = jnp.zeros((tile, tile), F32)
        for j in range(per_dev):
            code = info_ref[dev_h, j : j + 1, :]
            here = jnp.logical_and(code[:, :tile] == h, code[:, tile:] == t)
            total = total + jnp.where(here, every[dev_h, j], 0.0)
            code = info_ref[dev_t, j : j + 1, :]
            here = jnp.logical_and(code[:, :tile] == t, code[:, tile:] == h)
            total = total + jnp.where(here, flip[dev_t, j], 0.0)
        high, low = split(total)
        mat_h[chunk(h, tile), chunk(t, tile)] = high
        mat_l[chunk(h, tile), chunk(t, tile)] = low
        return carry

    lax.fori_loop(0, n_tiles * n_tiles, body, 0)


def column_kernel(n_vir, tiles_dev, info_in, occ_ref, vir_ref, blocks_ref, half_out, orb_out,
                  infos, every, flip, coef_ref, tab_h, tab_l, mat_h, mat_l, g_h, g_l,
                  away, near, own, half, y1, z1, y2, z2,
                  info_s, info_r, block_s, block_r, core_s, core_r, half_s,
                  y1_s, y1_r, z1_s, z1_r, y2_s, y2_r, z2_s, z2_r):
    n_grp, per_dev = every.shape[:2]
    n_occ = occ_ref.shape[0]
    width, rows = tab_h.shape
    mine = width // n_grp
    grp, pair = lax.axis_index("grp"), lax.axis_index("pair")
    core = lax.rem(pair, NC)
    y = lax.rem(lax.div(pair, NC), NY)
    z = lax.div(pair, NC * NY)

    def at(z_, y_, core_):
        return (grp, (z_ * NY + y_) * NC + core_)

    peers = [(lax.rem(grp + d, n_grp), pair) for d in range(1, n_grp)]
    peers += [at(z, y, 1 - core)]
    peers += [at(z, ring(y + s, NY), core) for s in (1, -1)]
    peers += [at(ring(z + s, NZ), y, core) for s in (1, -1)]
    barrier = pltpu.get_barrier_semaphore()
    for peer in peers:
        pl.semaphore_signal(barrier, inc=1, device_id=peer, device_id_type=MESH)
    pack_coef(occ_ref, vir_ref, coef_ref)
    infos[grp] = info_in[...]
    pl.semaphore_wait(barrier, len(peers))

    def over_x(src, dst, d, send, recv):
        return pltpu.make_async_remote_copy(
            src_ref=src, dst_ref=dst.at[grp], send_sem=send.at[d], recv_sem=recv.at[d],
            device_id=(lax.rem(grp + d, n_grp), pair), device_id_type=MESH)

    for d in (1, 3, 2):
        over_x(info_in, infos, d, info_s, info_r).start()
    for d in (1, 3, 2):
        over_x(blocks_ref, every, d, block_s, block_r).start()
    mine_copy = pltpu.make_async_copy(blocks_ref, every.at[grp], block_r.at[0])
    mine_copy.start()

    def tables(d, carry):
        g = lax.rem(grp + n_grp - d, n_grp)

        @pl.when(d > 0)
        def _():
            over_x(info_in, infos, d, info_s, info_r).wait_recv()

        table_part(infos, g, per_dev, coef_ref, tab_h, tab_l, n_occ, n_vir)
        return carry

    lax.fori_loop(0, n_grp, tables, 0)
    mine_copy.wait()
    for d in range(1, n_grp):
        over_x(blocks_ref, every, d, block_s, block_r).wait_recv()
    build_matrix(infos, every, flip, mat_h, mat_l, tiles_dev)
    share = chunk(grp, mine)

    def make_g(c, carry):
        cols = chunk(c)
        g = dot3(tab_h[share, :], tab_l[share, :], mat_h[:, cols], mat_l[:, cols], NN)
        g = g.reshape(NZ * NY, NC, SUB, STEP)
        for k in range(NC):
            g_h[k, :, cols], g_l[k, :, cols] = split(g[:, k].reshape(NZ * NY * SUB, STEP))
        return carry

    lax.fori_loop(0, rows // STEP, make_g, 0)
    parts = width // STEP // 2

    def product(which, side, c):
        tab = chunk(side * parts + c)
        p = dot3(g_h[which], g_l[which], tab_h[tab, :], tab_l[tab, :], NT)
        return p.reshape(NZ, NY, SUB, STEP)

    def over_core(side, c):
        return pltpu.make_async_remote_copy(
            src_ref=away.at[side, c], dst_ref=near.at[side, c], send_sem=core_s.at[side, c],
            recv_sem=core_r.at[side, c], device_id=at(z, y, 1 - core), device_id_type=MESH)

    def sibling(side):
        def body(c, carry):
            away[side, c] = product(1 - core, side, c)
            over_core(side, c).start()
            return carry

        lax.fori_loop(0, parts, body, 0)

    def kept(side, lo, hi):
        def body(c, carry):
            p = product(core, side, c)
            over_core(side, c).wait_recv()
            own[side, c] = p + near[side, c]
            return carry

        lax.fori_loop(lo, hi, body, 0)

    def part(h):
        return slice(h * parts // 2, (h + 1) * parts // 2)

    def chains(size, me, piece, landing, send, recv, to):
        return [
            [Chain(me, size, (1, -1)[d], lengths(size)[h][d], functools.partial(piece, h), landing.at[h, d],
                   send.at[h, d], recv.at[h, d], to) for d in range(2)]
            for h in range(2)
        ]

    to_y, to_z = (lambda v: at(z, v, core)), (lambda v: at(v, y, core))
    on_y1 = chains(NY, y, lambda h, v: own.at[1, part(h), :, v], y1, y1_s, y1_r, to_y)
    on_z2 = chains(NZ, z, lambda h, v: own.at[1, part(h), v, y], z2, z2_s, z2_r, to_z)
    on_z1 = chains(NZ, z, lambda h, v: own.at[0, part(h), v], z1, z1_s, z1_r, to_z)
    on_y2 = chains(NY, y, lambda h, v: own.at[0, part(h), z, v], y2, y2_s, y2_r, to_y)

    def start(pair_):
        for chain in pair_:
            chain.start()

    def advance(group, j):
        for chain in [c for pair_ in group for c in pair_]:
            chain.advance(j)

    def arrive(pair_, here):
        total = here[...]
        for chain in pair_:
            total = chain.arrive(total)
        return total

    def finish(side, h, pair_):
        total = arrive(pair_, own.at[side, part(h), z, y])
        for j in range(parts // 2):
            first = (side * parts + h * parts // 2 + j) * STEP
            orb_out[:, first : first + STEP] = total[j]

    local = chunk(grp, tiles_dev * (rows // n_grp // tiles_dev))

    def half_copy(c):
        return pltpu.make_async_copy(half.at[:, chunk(c)], half_out.at[:, chunk(c)], half_s.at[c])

    def half_part(lo, hi):
        def body(c, carry):
            tab = chunk(c)
            half[:, tab] = dot3(mat_h[local, :], mat_l[local, :], tab_h[tab, :], tab_l[tab, :], NT)
            half_copy(c).start()
            return carry

        lax.fori_loop(lo, hi, body, 0)

    sibling(1)
    kept(1, 0, parts // 2)
    start(on_y1[0])
    kept(1, parts // 2, parts)
    start(on_y1[1])
    sibling(0)
    advance(on_y1, 0)
    kept(0, 0, parts // 2)
    start(on_z1[0])
    kept(0, parts // 2, parts)
    start(on_z1[1])
    for h in range(2):
        here = own.at[1, part(h), :, y]
        here[...] = arrive(on_y1[h], here)
        start(on_z2[h])
    for j in range(max(max(lengths(NZ)[0]) - 1, 0)):
        half_part(2 * j, 2 * j + 2)
        advance(on_z1, j)
        advance(on_z2, j)
    half_part(2 * max(max(lengths(NZ)[0]) - 1, 0), width // STEP)
    for h in range(2):
        here = own.at[0, part(h), z]
        here[...] = arrive(on_z1[h], here)
        start(on_y2[h])
    for h in range(2):
        finish(1, h, on_z2[h])
    for j in range(max(lengths(NY)[0]) - 1):
        advance(on_y2, j)
    for h in range(2):
        finish(0, h, on_y2[h])

    for d in range(1, n_grp):
        over_x(info_in, infos, d, info_s, info_r).wait_send()
        over_x(blocks_ref, every, d, block_s, block_r).wait_send()
    for group in (on_y1, on_z1, on_y2, on_z2):
        for pair_ in group:
            for chain in pair_:
                chain.drain()

    def settle(c, carry):
        for side in range(2):
            over_core(side, c).wait_send()
            half_copy(side * parts + c).wait()
        return carry

    lax.fori_loop(0, parts, settle, 0)


def on_device(blocks, block_home, block_group, block_slot, pair_funcs, occ_coef, vir_coef):
    n_grp = lax.axis_size("grp")
    grp = lax.axis_index("grp")
    per_dev, tile, _ = blocks.shape
    rows_dev = pair_funcs.shape[1]
    tiles_dev = rows_dev // tile
    nb, n_occ = occ_coef.shape
    n_vir = vir_coef.shape[1]
    width = n_occ * n_vir
    rows = rows_dev * n_grp
    kept = NZ * NY * SUB
    parts = width // STEP // 2
    codes = [grp * tiles_dev + block_home, block_group[:, 0] * tiles_dev + block_slot]
    codes = jnp.concatenate([jnp.broadcast_to(c[:, None], (per_dev, tile)) for c in codes], axis=1)
    info = jnp.concatenate([codes, pair_funcs, jnp.zeros((INFO - per_dev - 2, rows_dev), I32)], axis=0)
    vmem = pl.BlockSpec(memory_space=pltpu.VMEM)
    hbm = pl.BlockSpec(memory_space=pl.ANY)
    dma = pltpu.SemaphoreType.DMA
    zh, yh = max(NZ // 2, 1), max(NY // 2, 1)
    return pl.pallas_call(
        functools.partial(column_kernel, n_vir, tiles_dev),
        out_shape=(jax.ShapeDtypeStruct((rows_dev, width), F32), jax.ShapeDtypeStruct((SUB, width), F32)),
        in_specs=[vmem, vmem, vmem, hbm],
        out_specs=(hbm, vmem),
        scratch_shapes=[
            pltpu.VMEM((n_grp, INFO, rows_dev), I32),
            pltpu.VMEM((n_grp, per_dev, tile, tile), F32),
            pltpu.VMEM((n_grp, per_dev, tile, tile), F32),
            pltpu.VMEM((2 * (n_occ + n_vir), nb), BF16),
            pltpu.VMEM((width, rows), BF16),
            pltpu.VMEM((width, rows), BF16),
            pltpu.VMEM((rows, rows), BF16),
            pltpu.VMEM((rows, rows), BF16),
            pltpu.VMEM((NC, kept, rows), BF16),
            pltpu.VMEM((NC, kept, rows), BF16),
            pltpu.VMEM((2, parts, NZ, NY, SUB, STEP), F32),
            pltpu.VMEM((2, parts, NZ, NY, SUB, STEP), F32),
            pltpu.VMEM((2, parts, NZ, NY, SUB, STEP), F32),
            pltpu.VMEM((rows_dev, width), F32),
            pltpu.VMEM((2, 2, yh, parts // 2, NZ, SUB, STEP), F32),
            pltpu.VMEM((2, 2, zh, parts // 2, NY, SUB, STEP), F32),
            pltpu.VMEM((2, 2, yh, parts // 2, SUB, STEP), F32),
            pltpu.VMEM((2, 2, zh, parts // 2, SUB, STEP), F32),
            dma((n_grp,)), dma((n_grp,)), dma((n_grp,)), dma((n_grp,)),
            dma((2, parts)), dma((2, parts)), dma((2 * parts,)),
            dma((2, 2, yh)), dma((2, 2, yh)), dma((2, 2, zh)), dma((2, 2, zh)),
            dma((2, 2, yh)), dma((2, 2, yh)), dma((2, 2, zh)), dma((2, 2, zh)),
        ],
        compiler_params=pltpu.CompilerParams(
            collective_id=0, has_side_effects=True, vmem_limit_bytes=56 * 2**20
        ),
    )(info, occ_coef.T, vir_coef, blocks)


def solution(mesh):
    both = ("grp", "pair")
    placed = (P(both, None, None), P(both), P(both, None), P(both), P(None, both), P(), P())
    return jax.shard_map(
        on_device,
        mesh=mesh,
        in_specs=placed,
        out_specs=(P(both, None), P(both, None)),
        check_vma=False,
    )
```

time: 275 us -> 75.2 us (0.27)
  waiting for transfers between devices: 203 us -> 0 us
  Pallas kernels: 30.5 us -> 67.7 us
  blocking collectives: 20.6 us -> 0 us
  between operations: 14.7 us -> 0.65 us
    unnamed x3 -> x0, waiting for transfers between devices: 196 us -> none
    pallas_call x1, Pallas kernels: 30.5 us -> 67.7 us  [on_device(): pl.pallas_call(functools.partial(column_kernel, n_vir, tiles_dev), out_sh...]
    all_gather x2 -> x0, blocking collectives: 20.6 us -> none  [the longest x1 10.9 us: on_device(): funcs = lax.all_gather(pair_funcs, 'grp', axis=1, tiled=True)]
    all_gather x1 -> x0, waiting for transfers between devices: 7.23 us -> none  [on_device(): every = lax.all_gather(blocks, 'grp', axis=0, tiled=True)]
  transfers between devices with their start and end apart: 2 -> 0, of which waited for: 2 -> 0; matrix products, arithmetic and copies ran while one was open for 1% -> 0% of each run, Pallas kernels for 0% -> 0%
where the time goes in v2:
time: 75.2 us; the launch traced here: 75 us
  Pallas kernels  67.7 us (90%)
  local copies, waits for them, and re-layouts  4.02 us (5%)
  other arithmetic  2.68 us (4%)
    pallas_call x1, Pallas kernels, on_device(): pl.pallas_call(functools.partial(column_kernel, n_vir, tiles_dev), out_sh...  67.7 us
    unnamed x4, local copies, waits for them, and re-layouts  3.8 us

profile of v2, /device:TPU:8, one launch (start us, length us, event | category | flops | bytes accessed | tf_op | source)
XLA Modules:
  0.0 75.0 jit_solution(8514997589468579444)
XLA Ops:
  0.6 0.7 broadcast_add_fusion
  1.3 0.7 bitcast_add_fusion
  2.0 0.1 pad.3.clone
  2.0 0.1 broadcast_in_dim.7
  2.1 0.1 broadcast_in_dim.6
  2.2 1.3 %add_add_fusion.info_in = s32[8,256]{1,0:T(8,128)} fusion(s32[2,256]{1,0:T(2,128)} %param.11, s32[4,128]{1,0:T(4,128)S(1)} %broadcast_in_dim.7, s32[4,128]{1,0:T(4,128)S(1)} %broadcast_in_dim.6, s32[8]{0:T(128)S(1)} %pad.3.clone), kind=kLoop, calls=%fused_computation | loop fusion | flops 6144 | bytes 14368 | tf_op jit(solution)/shard_map/concatenate | solution.py:344
  3.5 67.7 %shard_map.86 = (f32[256,2048]{1,0:T(8,128)}, f32[8,2048]{1,0:T(8,128)}) custom-call(s32[8,256]{1,0:T(8,128)} %add_add_fusion.info_in, f32[16,1536]{1,0:T(8,128)} %bitcast.3, f32[1536,128]{1,0:T(8,128)} %vir_ref.1, f32[4,128,128]{2,1,0:T(8,128)} %blocks_ref.1), custom_call_target="tpu_custom_call" | custom-call | tf_op jit(solution)/shard_map/pallas_call | solution.py:349
  71.2 0.0 copy-start
  71.2 3.2 %copy.11 = f32[256,2048]{1,0:T(8,128)} copy(f32[256,2048]{1,0:T(8,128)} %get-tuple-element.4) | data formatting | bytes 4194304
  74.4 0.0 copy-done
  74.4 0.6 copy.12
  (1 shorter events, 0.0 us)
Async XLA Ops:
  71.2 3.2 %copy-start = (f32[8,2048]{1,0:T(8,128)S(1)}, f32[8,2048]{1,0:T(8,128)}, u32[]{:S(2)}) copy-start(f32[8,2048]{1,0:T(8,128)} %get-tuple-element.5) | copy-start | bytes 196612

commit v3 on v2

v3 whole, which is shorter than its diff:
```python
import functools

import jax
import jax.numpy as jnp
from jax import lax
from jax.experimental import pallas as pl
from jax.experimental.pallas import tpu as pltpu
from jax.sharding import PartitionSpec as P

F32, BF16, I32 = jnp.float32, jnp.bfloat16, jnp.int32
NZ, NY, NC = 8, 4, 2
STEP = 256
SUB = 8
INFO = 8
WIDE = 512
VMEM_MIB = 56
MESH = pl.DeviceIdType.MESH
NN, NT = ((1,), (0,)), ((1,), (1,))


def split(value):
    high = value.astype(BF16)
    return high, (value - high.astype(F32)).astype(BF16)


def dot(lhs, rhs, contract):
    return lax.dot_general(lhs, rhs, (contract, ((), ())), preferred_element_type=F32)


def dot3(lh, ll, rh, rl, contract):
    return dot(lh, rh, contract) + (dot(lh, rl, contract) + dot(ll, rh, contract))


def chunk(c, step=STEP):
    return pl.ds(pl.multiple_of(c * step, step), step)


def ring(i, n):
    return lax.rem(i + 2 * n, n)


class Chain:
    def __init__(self, me, size, sign, length, piece, landing, send_sem, recv_sem, to):
        self.me, self.size, self.sign, self.length = me, size, sign, length
        self.piece, self.landing, self.send_sem, self.recv_sem, self.to = piece, landing, send_sem, recv_sem, to

    def owner(self, j):
        return ring(self.me + self.sign * (self.length - j), self.size)

    def copy(self, j):
        return pltpu.make_async_remote_copy(
            src_ref=self.piece(self.owner(j)),
            dst_ref=self.landing.at[j],
            send_sem=self.send_sem.at[j],
            recv_sem=self.recv_sem.at[j],
            device_id=self.to(ring(self.me + self.sign, self.size)),
            device_id_type=MESH,
        )

    def start(self):
        if self.length:
            self.copy(0).start()

    def advance(self, j):
        if j < self.length - 1:
            self.copy(j).wait_recv()
            here = self.piece(self.owner(j + 1))
            here[...] = here[...] + self.landing[j]
            self.copy(j + 1).start()

    def arrive(self, total):
        if not self.length:
            return total
        self.copy(self.length - 1).wait_recv()
        return total + self.landing[self.length - 1]

    def drain(self):
        for j in range(self.length):
            self.copy(j).wait_send()


def lengths(n):
    far, near = n // 2, n - 1 - n // 2
    return ((far, near), (near, far))


def pack_coef(occ_ref, vir_ref, coef_ref):
    n_occ, n_vir = occ_ref.shape[0], vir_ref.shape[1]
    width = n_vir + n_occ
    coef_ref[:n_vir], coef_ref[width : width + n_vir] = split(vir_ref[...].T)
    coef_ref[n_vir:width], coef_ref[width + n_vir :] = split(occ_ref[...])


def table_part(info_ref, g, first, coef_ref, tab_h, tab_l, n_occ, n_vir):
    nb = coef_ref.shape[1]
    width = n_vir + n_occ
    got = []
    for f in range(2):
        func = info_ref[g, first + f : first + f + 1, :]
        hot = lax.broadcasted_iota(I32, (nb, STEP), 0) == func
        hot = jnp.where(hot, 1.0, 0.0).astype(BF16)
        both = dot(coef_ref[...], hot, NN)
        got.append(both[:width] + both[width:])
    (vir_p, occ_p), (vir_q, occ_q) = [(v[:n_vir], v[n_vir:]) for v in got]
    cols = chunk(g)
    for i in range(n_occ):
        entry = occ_p[i : i + 1] * vir_q + occ_q[i : i + 1] * vir_p
        high, low = split(entry)
        tab_h[i * n_vir : (i + 1) * n_vir, cols] = high
        tab_l[i * n_vir : (i + 1) * n_vir, cols] = low


def build_matrix(info_ref, every, flip, mat_h, mat_l, tiles_dev):
    n_grp, per_dev, tile, _ = every.shape
    n_tiles = n_grp * tiles_dev
    def body(step, carry):
        h, t = lax.div(step, n_tiles), lax.rem(step, n_tiles)
        dev_h, dev_t = lax.div(h, tiles_dev), lax.div(t, tiles_dev)
        total = jnp.zeros((tile, tile), F32)
        for j in range(per_dev):
            code = info_ref[dev_h, j : j + 1, :]
            here = jnp.logical_and(code[:, :tile] == h, code[:, tile:] == t)
            total = total + jnp.where(here, every[dev_h, j], 0.0)
            code = info_ref[dev_t, j : j + 1, :]
            here = jnp.logical_and(code[:, :tile] == t, code[:, tile:] == h)
            total = total + jnp.where(here, flip[dev_t, j], 0.0)
        high, low = split(total)
        mat_h[chunk(h, tile), chunk(t, tile)] = high
        mat_l[chunk(h, tile), chunk(t, tile)] = low
        return carry

    lax.fori_loop(0, n_tiles * n_tiles, body, 0)


class Direct:
    def __init__(self, me, size, piece, landing, send_sem, recv_sem, to):
        self.me, self.size, self.piece, self.landing = me, size, piece, landing
        self.send_sem, self.recv_sem, self.to = send_sem, recv_sem, to

    def copy(self, d):
        peer = ring(self.me + d, self.size)
        return pltpu.make_async_remote_copy(
            src_ref=self.piece(peer),
            dst_ref=self.landing.at[d],
            send_sem=self.send_sem.at[d],
            recv_sem=self.recv_sem.at[d],
            device_id=self.to(peer),
            device_id_type=MESH,
        )

    def order(self):
        return sorted(range(1, self.size), key=lambda d: -min(d, self.size - d))

    def start(self):
        for d in self.order():
            self.copy(d).start()

    def arrive(self, total):
        for d in reversed(self.order()):
            self.copy(d).wait_recv()
            total = total + self.landing[d]
        return total

    def drain(self):
        for d in range(1, self.size):
            self.copy(d).wait_send()


def column_kernel(n_vir, tiles_dev, home_in, group_in, slot_in, funcs_in, occ_in, vir_in, blocks_ref,
                  half_out, orb_out, home_ref, group_ref, slot_ref, funcs_ref, occ_ref, vir_ref, infos, every, flip, coef_ref, tab_h, tab_l, mat_h, mat_l, g_h, g_l,
                  away, near, own, half, y1, z1, y2, z2,
                  info_s, info_r, block_s, block_r, own_s, core_s, core_r, half_s,
                  y1_s, y1_r, z1_s, z1_r, y2_s, y2_r, z2_s, z2_r):
    n_grp, per_dev, tile, _ = every.shape
    n_occ = occ_ref.shape[0]
    width, rows = tab_h.shape
    mine = width // n_grp
    grp, pair = lax.axis_index("grp"), lax.axis_index("pair")
    core = lax.rem(pair, NC)
    y = lax.rem(lax.div(pair, NC), NY)
    z = lax.div(pair, NC * NY)
    right, left = ring(grp + 1, n_grp), ring(grp - 1, n_grp)
    far = ring(grp + 2, n_grp)

    def at(z_, y_, core_):
        return (grp, (z_ * NY + y_) * NC + core_)

    def to_y(v):
        return at(z, v, core)

    def to_z(v):
        return at(v, y, core)

    peers = [(ring(grp + d, n_grp), pair) for d in range(1, n_grp)]
    peers += [at(z, y, 1 - core)]
    peers += [to_y(ring(y + d, NY)) for d in range(1, NY)]
    peers += [to_z(ring(z + d, NZ)) for d in range(1, NZ)]
    pairs = ((home_in, home_ref), (group_in, group_ref), (slot_in, slot_ref), (funcs_in, funcs_ref),
             (occ_in, occ_ref), (vir_in, vir_ref))
    fetches = [pltpu.make_async_copy(src, dst, own_s.at[1 + i]) for i, (src, dst) in enumerate(pairs)]
    for fetch in fetches:
        fetch.start()
    barrier = pltpu.get_barrier_semaphore()
    for peer in peers:
        pl.semaphore_signal(barrier, inc=1, device_id=peer, device_id_type=MESH)
    for fetch in fetches[:4]:
        fetch.wait()
    lane = lax.broadcasted_iota(I32, (1, STEP), 1)
    for j in range(per_dev):
        home = grp * tiles_dev + home_ref[j]
        partner = group_ref[j] * tiles_dev + slot_ref[j]
        infos[grp, j : j + 1, :] = jnp.where(lane < tile, home, partner)
    infos[grp, per_dev : per_dev + 2, :] = funcs_ref[...]
    infos[grp, per_dev + 2 :, :] = jnp.zeros((INFO - per_dev - 2, STEP), I32)
    pl.semaphore_wait(barrier, len(peers))

    def tell(d):
        return pltpu.make_async_remote_copy(
            src_ref=infos.at[grp], dst_ref=infos.at[grp], send_sem=info_s.at[d], recv_sem=info_r.at[d],
            device_id=(ring(grp + d, n_grp), pair), device_id_type=MESH)

    split_at = per_dev // 2
    parts_of = (slice(0, split_at), slice(split_at, per_dev))

    def pass_on(way, step):
        to = (right, left)[way]
        which = parts_of[way if step != 1 else 1 - way]
        if step < 2:
            src, dst = blocks_ref.at[which], every.at[grp, which]
        else:
            src = dst = every.at[(left, right)[way], which]
        return pltpu.make_async_remote_copy(
            src_ref=src, dst_ref=dst, send_sem=block_s.at[way, step], recv_sem=block_r.at[way, step],
            device_id=(to, pair), device_id_type=MESH)

    for d in (1, 3, 2):
        tell(d).start()
    for step in range(2):
        for way in range(2):
            pass_on(way, step).start()
    mine_copy = pltpu.make_async_copy(blocks_ref, every.at[grp], own_s.at[0])
    mine_copy.start()
    for fetch in fetches[4:]:
        fetch.wait()
    pack_coef(occ_ref, vir_ref, coef_ref)

    def tables(d, carry):
        g = ring(grp - d, n_grp)

        @pl.when(d > 0)
        def _():
            tell(d).wait_recv()

        table_part(infos, g, per_dev, coef_ref, tab_h, tab_l, n_occ, n_vir)
        return carry

    lax.fori_loop(0, n_grp, tables, 0)
    for way in range(2):
        pass_on(way, 0).wait_recv()
        pass_on(way, 2).start()

    def turn(g, which):
        for j in range(which.start, which.stop):
            flip[g, j] = every[g, j].T

    mine_copy.wait()
    turn(grp, slice(0, per_dev))
    for way in range(2):
        pass_on(way, 1).wait_recv()
        turn((left, right)[way], slice(0, per_dev))
    for way in range(2):
        pass_on(way, 2).wait_recv()
        turn(far, parts_of[way])
    build_matrix(infos, every, flip, mat_h, mat_l, tiles_dev)
    share = chunk(grp, mine)

    def make_g(c, carry):
        cols = chunk(c, WIDE)
        g = dot3(tab_h[share, :], tab_l[share, :], mat_h[:, cols], mat_l[:, cols], NN)
        g = g.reshape(NZ * NY, NC, SUB, WIDE)
        for k in range(NC):
            kept = lax.rem(core + k + 1, NC)
            g_h[kept, :, cols], g_l[kept, :, cols] = split(g[:, k].reshape(NZ * NY * SUB, WIDE))
        return carry

    lax.fori_loop(0, rows // WIDE, make_g, 0)
    pieces = width // WIDE

    def over_core(p):
        return pltpu.make_async_remote_copy(
            src_ref=away.at[p], dst_ref=near.at[p], send_sem=core_s.at[p], recv_sem=core_r.at[p],
            device_id=at(z, y, 1 - core), device_id_type=MESH)

    def produce(p):
        tab = slice(p * WIDE, (p + 1) * WIDE)
        value = dot3(g_h[...].reshape(-1, rows), g_l[...].reshape(-1, rows), tab_h[tab, :], tab_l[tab, :], NT)
        value = value.reshape(NC, NZ, NY, SUB, WIDE)
        away[p] = value[0]
        own[p] = value[1]
        over_core(p).start()

    def settle(p):
        over_core(p).wait_recv()
        own[p] = own[p] + near[p]

    def chains(p, size, me, piece, landing, send, recv, to):
        hops = lengths(size)[p // 2 % 2]
        return [Chain(me, size, (1, -1)[d], hops[d], piece, landing.at[d], send.at[d], recv.at[d], to)
                for d in range(2)]

    first, second = [], []
    for p in range(pieces):
        i = p // 2
        if p % 2 == 0:
            first.append(chains(p, NZ, z, lambda v, p=p: own.at[p, v], z1.at[i], z1_s.at[i], z1_r.at[i], to_z))
            second.append([Direct(y, NY, lambda v, p=p: own.at[p, z, v], y2.at[i], y2_s.at[i], y2_r.at[i], to_y)])
        else:
            first.append(chains(p, NY, y, lambda v, p=p: own.at[p, :, v], y1.at[i], y1_s.at[i], y1_r.at[i], to_y))
            second.append([Direct(z, NZ, lambda v, p=p: own.at[p, v, y], z2.at[i], z2_s.at[i], z2_r.at[i], to_z)])

    def start(group):
        for way in group:
            way.start()

    def advance(p, j):
        for way in first[p]:
            way.advance(j)

    def turn_corner(p):
        here = own.at[p, z] if p % 2 == 0 else own.at[p, :, y]
        total = here[...]
        for way in first[p]:
            total = way.arrive(total)
        here[...] = total
        start(second[p])

    def finish(p):
        total = own[p, z, y]
        for way in second[p]:
            total = way.arrive(total)
        orb_out[:, p * WIDE : (p + 1) * WIDE] = total

    local = chunk(grp, rows // n_grp)

    def half_copy(c):
        cols = slice(c * WIDE, (c + 1) * WIDE)
        return pltpu.make_async_copy(half.at[:, cols], half_out.at[:, cols], half_s.at[c])

    def half_part(c):
        tab = slice(c * WIDE, (c + 1) * WIDE)
        half[:, tab] = dot3(mat_h[local, :], mat_l[local, :], tab_h[tab, :], tab_l[tab, :], NT)
        half_copy(c).start()

    produce(0)
    produce(1)
    settle(0)
    start(first[0])
    produce(2)
    settle(1)
    start(first[1])
    advance(0, 0)
    produce(3)
    settle(2)
    start(first[2])
    advance(1, 0)
    advance(0, 1)
    half_part(0)
    settle(3)
    start(first[3])
    half_part(1)
    advance(0, 2)
    advance(2, 0)
    half_part(2)
    turn_corner(1)
    advance(3, 0)
    advance(2, 1)
    half_part(3)
    turn_corner(0)
    advance(2, 2)
    turn_corner(3)
    turn_corner(2)
    for p in (1, 0, 3, 2):
        finish(p)

    for d in range(1, n_grp):
        tell(d).wait_send()
    for way in range(2):
        for step in range(3):
            pass_on(way, step).wait_send()
    for group in first + second:
        for way in group:
            way.drain()
    for p in range(pieces):
        over_core(p).wait_send()
        half_copy(p).wait()


def on_device(blocks, block_home, block_group, block_slot, pair_funcs, occ_coef, vir_coef):
    n_grp = lax.axis_size("grp")
    per_dev, tile, _ = blocks.shape
    rows_dev = pair_funcs.shape[1]
    tiles_dev = rows_dev // tile
    nb, n_occ = occ_coef.shape
    n_vir = vir_coef.shape[1]
    width = n_occ * n_vir
    rows = rows_dev * n_grp
    kept = NZ * NY * SUB
    pieces = width // WIDE
    vmem = pl.BlockSpec(memory_space=pltpu.VMEM)
    hbm = pl.BlockSpec(memory_space=pltpu.HBM)
    anywhere = pl.BlockSpec(memory_space=pl.ANY)
    dma = pltpu.SemaphoreType.DMA
    some = pieces // 2
    zh, yh = max(NZ // 2, 1), max(NY // 2, 1)
    return pl.pallas_call(
        functools.partial(column_kernel, n_vir, tiles_dev),
        out_shape=(jax.ShapeDtypeStruct((rows_dev, width), F32), jax.ShapeDtypeStruct((SUB, width), F32)),
        in_specs=[hbm] * 7,
        out_specs=(anywhere, vmem),
        scratch_shapes=[
            pltpu.SMEM((per_dev,), I32),
            pltpu.SMEM((per_dev,), I32),
            pltpu.SMEM((per_dev,), I32),
            pltpu.VMEM((2, rows_dev), I32),
            pltpu.VMEM((n_occ, nb), F32),
            pltpu.VMEM((nb, n_vir), F32),
            pltpu.VMEM((n_grp, INFO, rows_dev), I32),
            pltpu.VMEM((n_grp, per_dev, tile, tile), F32),
            pltpu.VMEM((n_grp, per_dev, tile, tile), F32),
            pltpu.VMEM((2 * (n_occ + n_vir), nb), BF16),
            pltpu.VMEM((width, rows), BF16),
            pltpu.VMEM((width, rows), BF16),
            pltpu.VMEM((rows, rows), BF16),
            pltpu.VMEM((rows, rows), BF16),
            pltpu.VMEM((NC, kept, rows), BF16),
            pltpu.VMEM((NC, kept, rows), BF16),
            pltpu.VMEM((pieces, NZ, NY, SUB, WIDE), F32),
            pltpu.VMEM((pieces, NZ, NY, SUB, WIDE), F32),
            pltpu.VMEM((pieces, NZ, NY, SUB, WIDE), F32),
            pltpu.VMEM((rows_dev, width), F32),
            pltpu.VMEM((some, 2, yh, NZ, SUB, WIDE), F32),
            pltpu.VMEM((some, 2, zh, NY, SUB, WIDE), F32),
            pltpu.VMEM((some, NY, SUB, WIDE), F32),
            pltpu.VMEM((some, NZ, SUB, WIDE), F32),
            dma((n_grp,)), dma((n_grp,)), dma((2, 3)), dma((2, 3)), dma((7,)),
            dma((pieces,)), dma((pieces,)), dma((pieces,)),
            dma((some, 2, yh)), dma((some, 2, yh)), dma((some, 2, zh)), dma((some, 2, zh)),
            dma((some, NY)), dma((some, NY)), dma((some, NZ)), dma((some, NZ)),
        ],
        compiler_params=pltpu.CompilerParams(
            collective_id=0, has_side_effects=True, vmem_limit_bytes=VMEM_MIB * 2**20
        ),
    )(block_home, block_group.reshape(per_dev), block_slot, pair_funcs, occ_coef.T, vir_coef, blocks)


def solution(mesh):
    both = ("grp", "pair")
    placed = (P(both, None, None), P(both), P(both, None), P(both), P(None, both), P(), P())
    return jax.shard_map(
        on_device,
        mesh=mesh,
        in_specs=placed,
        out_specs=(P(both, None), P(both, None)),
        check_vma=False,
    )
```

time: 75.2 us -> 65.8 us (0.87); the launches traced: 75 us -> 64.8 us
  Pallas kernels: 67.7 us -> 60.3 us
  other arithmetic: 2.68 us -> 0 us
    pallas_call x1, Pallas kernels: 67.7 us -> 60.3 us  [on_device(): pl.pallas_call(functools.partial(column_kernel, n_vir, tiles_dev), out_sh...]
    concatenate x1 -> x0, other arithmetic: 1.35 us -> none  [on_device(): jnp.concatenate([codes, pair_funcs, jnp.zeros((INFO - per_dev - 2, rows_d...]
    add x2 -> x0, other arithmetic: 1.33 us -> none  [the longest x1 0.67 us: on_device(): block_group[:, 0] * tiles_dev + block_slot]
where the time goes in v3:
time: 65.8 us; the launch traced here: 64.8 us
  Pallas kernels  60.3 us (92%)
  local copies, waits for them, and re-layouts  3.8 us (6%)
    pallas_call x1, Pallas kernels, on_device(): pl.pallas_call(functools.partial(column_kernel, n_vir, tiles_dev), out_sh...  60.3 us
    unnamed x4, local copies, waits for them, and re-layouts  3.8 us

profile of v3, /device:TPU:8, one launch (start us, length us, event | category | flops | bytes accessed | tf_op | source)
XLA Modules:
  0.0 64.8 jit_solution(11605925276019864241)
XLA Ops:
  0.6 60.3 %shard_map.86 = (f32[256,2048]{1,0:T(8,128)}, f32[8,2048]{1,0:T(8,128)}) custom-call(s32[4]{0:T(128)} %home_in.1, s32[4]{0:T(128)} %bitcast.3, s32[4]{0:T(128)} %slot_in.1, s32[2,256]{1,0:T(2,128)} %funcs_in.1, f32[16,1536]{1,0:T(8,128)} %bitcast.2, f32[1536,128]{1,0:T(8,128)} %vir_in.1, f32[4,128,128]{2,1,0:T(8,128)} %blocks_ref.1), custom_call_target="tpu_custom_call" | custom-call | tf_op jit(solution)/shard_map/pallas_call | solution.py:415
  60.9 0.0 copy-start
  61.0 3.2 %copy.11 = f32[256,2048]{1,0:T(8,128)} copy(f32[256,2048]{1,0:T(8,128)} %get-tuple-element.4) | data formatting | bytes 4194304
  64.1 0.0 copy-done
  64.1 0.6 copy.12
Async XLA Ops:
  60.9 3.2 %copy-start = (f32[8,2048]{1,0:T(8,128)S(1)}, f32[8,2048]{1,0:T(8,128)}, u32[]{:S(2)}) copy-start(f32[8,2048]{1,0:T(8,128)} %get-tuple-element.5) | copy-start | bytes 196612

commit v4 on v3

--- a/solution.py
+++ b/solution.py
@@ -12,7 +12,9 @@
 STEP = 256
 SUB = 8
 INFO = 8
-WIDE = 512
+WIDE = 256
+OWN = 1
+HALVES = 4
 VMEM_MIB = 56
 MESH = pl.DeviceIdType.MESH
 NN, NT = ((1,), (0,)), ((1,), (1,))
@@ -110,26 +112,22 @@
         tab_l[i * n_vir : (i + 1) * n_vir, cols] = low
 
 
-def build_matrix(info_ref, every, flip, mat_h, mat_l, tiles_dev):
-    n_grp, per_dev, tile, _ = every.shape
-    n_tiles = n_grp * tiles_dev
-    def body(step, carry):
-        h, t = lax.div(step, n_tiles), lax.rem(step, n_tiles)
-        dev_h, dev_t = lax.div(h, tiles_dev), lax.div(t, tiles_dev)
-        total = jnp.zeros((tile, tile), F32)
-        for j in range(per_dev):
-            code = info_ref[dev_h, j : j + 1, :]
-            here = jnp.logical_and(code[:, :tile] == h, code[:, tile:] == t)
-            total = total + jnp.where(here, every[dev_h, j], 0.0)
-            code = info_ref[dev_t, j : j + 1, :]
-            here = jnp.logical_and(code[:, :tile] == t, code[:, tile:] == h)
-            total = total + jnp.where(here, flip[dev_t, j], 0.0)
-        high, low = split(total)
-        mat_h[chunk(h, tile), chunk(t, tile)] = high
-        mat_l[chunk(h, tile), chunk(t, tile)] = low
-        return carry
-
-    lax.fori_loop(0, n_tiles * n_tiles, body, 0)
+def build_tile(info_ref, every, flip, mat_h, mat_l, tiles_dev, group_of, h, t):
+    _, per_dev, tile, _ = every.shape
+    dev_h, dev_t = lax.div(h, tiles_dev), lax.div(t, tiles_dev)
+    tile_h = group_of(dev_h) * tiles_dev + lax.rem(h, tiles_dev)
+    tile_t = group_of(dev_t) * tiles_dev + lax.rem(t, tiles_dev)
+    total = jnp.zeros((tile, tile), F32)
+    for j in range(per_dev):
+        code = info_ref[dev_h, j : j + 1, :]
+        here = jnp.logical_and(code[:, :tile] == tile_h, code[:, tile:] == tile_t)
+        total = total + jnp.where(here, every[dev_h, j], 0.0)
+        code = info_ref[dev_t, j : j + 1, :]
+        here = jnp.logical_and(code[:, :tile] == tile_t, code[:, tile:] == tile_h)
+        total = total + jnp.where(here, flip[dev_t, j], 0.0)
+    high, low = split(total)
+    mat_h[chunk(h, tile), chunk(t, tile)] = high
+    mat_l[chunk(h, tile), chunk(t, tile)] = low
 
 
 class Direct:
@@ -167,10 +165,10 @@
 
 
 def column_kernel(n_vir, tiles_dev, home_in, group_in, slot_in, funcs_in, occ_in, vir_in, blocks_ref,
-                  half_out, orb_out, home_ref, group_ref, slot_ref, funcs_ref, occ_ref, vir_ref, infos, every, flip, coef_ref, tab_h, tab_l, mat_h, mat_l, g_h, g_l,
-                  away, near, own, half, y1, z1, y2, z2,
+                  half_out, orb_out, home_ref, group_ref, slot_ref, funcs_ref, occ_ref, vir_ref, infos, every, flip, coef_ref, tab_h, tab_l, mat_h, mat_l, g_sum, g_h, g_l,
+                  away, near, own_z, own_y, half, y1, z1, y2, z2, zc,
                   info_s, info_r, block_s, block_r, own_s, core_s, core_r, half_s,
-                  y1_s, y1_r, z1_s, z1_r, y2_s, y2_r, z2_s, z2_r):
+                  y1_s, y1_r, z1_s, z1_r, y2_s, y2_r, z2_s, z2_r, zc_s, zc_r):
     n_grp, per_dev, tile, _ = every.shape
     n_occ = occ_ref.shape[0]
     width, rows = tab_h.shape
@@ -180,7 +178,9 @@
     y = lax.rem(lax.div(pair, NC), NY)
     z = lax.div(pair, NC * NY)
     right, left = ring(grp + 1, n_grp), ring(grp - 1, n_grp)
-    far = ring(grp + 2, n_grp)
+
+    def group_of(slot):
+        return ring(grp + OWN - slot, n_grp)
 
     def at(z_, y_, core_):
         return (grp, (z_ * NY + y_) * NC + core_)
@@ -209,14 +209,14 @@
     for j in range(per_dev):
         home = grp * tiles_dev + home_ref[j]
         partner = group_ref[j] * tiles_dev + slot_ref[j]
-        infos[grp, j : j + 1, :] = jnp.where(lane < tile, home, partner)
-    infos[grp, per_dev : per_dev + 2, :] = funcs_ref[...]
-    infos[grp, per_dev + 2 :, :] = jnp.zeros((INFO - per_dev - 2, STEP), I32)
+        infos[OWN, j : j + 1, :] = jnp.where(lane < tile, home, partner)
+    infos[OWN, per_dev : per_dev + 2, :] = funcs_ref[...]
+    infos[OWN, per_dev + 2 :, :] = jnp.zeros((INFO - per_dev - 2, STEP), I32)
     pl.semaphore_wait(barrier, len(peers))
 
     def tell(d):
         return pltpu.make_async_remote_copy(
-            src_ref=infos.at[grp], dst_ref=infos.at[grp], send_sem=info_s.at[d], recv_sem=info_r.at[d],
+            src_ref=infos.at[OWN], dst_ref=infos.at[ring(OWN + d, n_grp)], send_sem=info_s.at[d], recv_sem=info_r.at[d],
             device_id=(ring(grp + d, n_grp), pair), device_id_type=MESH)
 
     split_at = per_dev // 2
@@ -226,9 +226,9 @@
         to = (right, left)[way]
         which = parts_of[way if step != 1 else 1 - way]
         if step < 2:
-            src, dst = blocks_ref.at[which], every.at[grp, which]
+            src, dst = blocks_ref.at[which], every.at[(OWN + 1, OWN - 1)[way], which]
         else:
-            src = dst = every.at[(left, right)[way], which]
+            src, dst = every.at[(OWN + 1, OWN - 1)[way], which], every.at[OWN + 2, which]
         return pltpu.make_async_remote_copy(
             src_ref=src, dst_ref=dst, send_sem=block_s.at[way, step], recv_sem=block_r.at[way, step],
             device_id=(to, pair), device_id_type=MESH)
@@ -238,20 +238,20 @@
     for step in range(2):
         for way in range(2):
             pass_on(way, step).start()
-    mine_copy = pltpu.make_async_copy(blocks_ref, every.at[grp], own_s.at[0])
+    mine_copy = pltpu.make_async_copy(blocks_ref, every.at[OWN], own_s.at[0])
     mine_copy.start()
     for fetch in fetches[4:]:
         fetch.wait()
     pack_coef(occ_ref, vir_ref, coef_ref)
 
     def tables(d, carry):
-        g = ring(grp - d, n_grp)
+        slot = ring(OWN + d, n_grp)
 
         @pl.when(d > 0)
         def _():
             tell(d).wait_recv()
 
-        table_part(infos, g, per_dev, coef_ref, tab_h, tab_l, n_occ, n_vir)
+        table_part(infos, slot, per_dev, coef_ref, tab_h, tab_l, n_occ, n_vir)
         return carry
 
     lax.fori_loop(0, n_grp, tables, 0)
@@ -263,136 +263,211 @@
         for j in range(which.start, which.stop):
             flip[g, j] = every[g, j].T
 
+    n_tiles = rows // tile
+    close = (OWN + 2) * tiles_dev
+    rest = slice(close * tile, rows)
+    share = chunk(grp, mine)
+
+    def build(count_t, first_h, first_t):
+        def body(step, carry):
+            h, t = first_h + lax.div(step, count_t), first_t + lax.rem(step, count_t)
+            build_tile(infos, every, flip, mat_h, mat_l, tiles_dev, group_of, h, t)
+            return carry
+
+        return body
+
     mine_copy.wait()
-    turn(grp, slice(0, per_dev))
+    turn(OWN, slice(0, per_dev))
     for way in range(2):
         pass_on(way, 1).wait_recv()
-        turn((left, right)[way], slice(0, per_dev))
+        turn((OWN + 1, OWN - 1)[way], slice(0, per_dev))
+    lax.fori_loop(0, close * close, build(close, 0, 0), 0)
+
+    def first_g(c, carry):
+        cols = chunk(c)
+        g_sum[:, cols] = dot3(tab_h[share, : close * tile], tab_l[share, : close * tile],
+                              mat_h[: close * tile, cols], mat_l[: close * tile, cols], NN)
+        return carry
+
+    lax.fori_loop(0, close * tile // STEP, first_g, 0)
+
+    def keep_g(g, cols):
+        g = g.reshape(NZ * NY, NC, SUB, STEP)
+        for k in range(NC):
+            kept = lax.rem(core + k + 1, NC)
+            g_h[kept, :, cols], g_l[kept, :, cols] = split(g[:, k].reshape(NZ * NY * SUB, STEP))
+
     for way in range(2):
         pass_on(way, 2).wait_recv()
-        turn(far, parts_of[way])
-    build_matrix(infos, every, flip, mat_h, mat_l, tiles_dev)
-    share = chunk(grp, mine)
-
-    def make_g(c, carry):
-        cols = chunk(c, WIDE)
-        g = dot3(tab_h[share, :], tab_l[share, :], mat_h[:, cols], mat_l[:, cols], NN)
-        g = g.reshape(NZ * NY, NC, SUB, WIDE)
-        for k in range(NC):
-            kept = lax.rem(core + k + 1, NC)
-            g_h[kept, :, cols], g_l[kept, :, cols] = split(g[:, k].reshape(NZ * NY * SUB, WIDE))
+        turn(OWN + 2, parts_of[way])
+    lax.fori_loop(0, (n_tiles - close) * n_tiles, build(n_tiles, close, 0), 0)
+    lax.fori_loop(0, close * (n_tiles - close), build(n_tiles - close, 0, close), 0)
+
+    def second_g(c, carry):
+        cols = chunk(c)
+        keep_g(g_sum[:, cols] + dot3(tab_h[share, rest], tab_l[share, rest], mat_h[rest, cols], mat_l[rest, cols], NN), cols)
         return carry
 
-    lax.fori_loop(0, rows // WIDE, make_g, 0)
-    pieces = width // WIDE
+    lax.fori_loop(0, close * tile // STEP, second_g, 0)
+    keep_g(dot3(tab_h[share, :], tab_l[share, :], mat_h[:, rest], mat_l[:, rest], NN), rest)
 
     def over_core(p):
         return pltpu.make_async_remote_copy(
             src_ref=away.at[p], dst_ref=near.at[p], send_sem=core_s.at[p], recv_sem=core_r.at[p],
             device_id=at(z, y, 1 - core), device_id_type=MESH)
 
-    def produce(p):
-        tab = slice(p * WIDE, (p + 1) * WIDE)
+    pieces = width // WIDE
+    some = pieces // 2
+
+    def produce(p, own_ref, i):
+        tab = chunk(p)
         value = dot3(g_h[...].reshape(-1, rows), g_l[...].reshape(-1, rows), tab_h[tab, :], tab_l[tab, :], NT)
         value = value.reshape(NC, NZ, NY, SUB, WIDE)
         away[p] = value[0]
-        own[p] = value[1]
+        own_ref[i] = value[1]
         over_core(p).start()
 
-    def settle(p):
+    def settle(p, own_ref, i):
         over_core(p).wait_recv()
-        own[p] = own[p] + near[p]
-
-    def chains(p, size, me, piece, landing, send, recv, to):
-        hops = lengths(size)[p // 2 % 2]
-        return [Chain(me, size, (1, -1)[d], hops[d], piece, landing.at[d], send.at[d], recv.at[d], to)
-                for d in range(2)]
-
-    first, second = [], []
-    for p in range(pieces):
-        i = p // 2
-        if p % 2 == 0:
-            first.append(chains(p, NZ, z, lambda v, p=p: own.at[p, v], z1.at[i], z1_s.at[i], z1_r.at[i], to_z))
-            second.append([Direct(y, NY, lambda v, p=p: own.at[p, z, v], y2.at[i], y2_s.at[i], y2_r.at[i], to_y)])
-        else:
-            first.append(chains(p, NY, y, lambda v, p=p: own.at[p, :, v], y1.at[i], y1_s.at[i], y1_r.at[i], to_y))
-            second.append([Direct(z, NZ, lambda v, p=p: own.at[p, v, y], z2.at[i], z2_s.at[i], z2_r.at[i], to_z)])
+        own_ref[i] = own_ref[i] + near[p]
+
+    def both_ways(i, size, me, piece, landing, send, recv, to):
+        side = 1 - 2 * lax.rem(i, 2) if isinstance(i, jax.Array) else 1 - 2 * (i % 2)
+        return [Chain(me, size, side * (1, -1)[d], lengths(size)[0][d], piece, landing.at[i, d], send.at[i, d],
+                      recv.at[i, d], to) for d in range(2)]
+
+    def round_z(i):
+        return both_ways(i, NZ, z, lambda v: own_z.at[i, v], z1, z1_s, z1_r, to_z)
+
+    def round_y(i):
+        return both_ways(i, NY, y, lambda v: own_y.at[i, :, v], y1, y1_s, y1_r, to_y)
 
     def start(group):
         for way in group:
             way.start()
 
-    def advance(p, j):
-        for way in first[p]:
+    def advance(group, j):
+        for way in group:
             way.advance(j)
 
-    def turn_corner(p):
-        here = own.at[p, z] if p % 2 == 0 else own.at[p, :, y]
-        total = here[...]
-        for way in first[p]:
+    def arrive(group, total):
+        for way in group:
             total = way.arrive(total)
-        here[...] = total
-        start(second[p])
-
-    def finish(p):
-        total = own[p, z, y]
-        for way in second[p]:
-            total = way.arrive(total)
-        orb_out[:, p * WIDE : (p + 1) * WIDE] = total
-
-    local = chunk(grp, rows // n_grp)
+        return total
+
+    def end_z(i):
+        own_z[i, z] = arrive(round_z(i), own_z[i, z])
+
+    def end_y(i):
+        own_y[i, :, y] = arrive(round_y(i), own_y[i, :, y])
+
+    def two(b):
+        return slice(2 * b, 2 * b + 2)
+
+    last_y = [Direct(y, NY, lambda v, b=b: own_z.at[two(b), z, v], y2.at[b], y2_s.at[b], y2_r.at[b], to_y)
+              for b in range(some // 2)]
+    last_z = Direct(z, NZ, lambda v: own_y.at[two(1), v, y], z2, z2_s, z2_r, to_z)
+    chain_z = [Chain(z, NZ, (1, -1)[d], lengths(NZ)[0][d], lambda v: own_y.at[two(0), v, y], zc.at[d], zc_s.at[d],
+                     zc_r.at[d], to_z) for d in range(2)]
+
+    def give(side, b, group):
+        total = arrive(group, (own_z, own_y)[side][two(b), z, y])
+        for i in range(2):
+            first = (2 * (2 * b + i) + side) * WIDE
+            orb_out[:, first : first + WIDE] = total[i]
+
+    local = slice(OWN * (rows // n_grp), (OWN + 1) * (rows // n_grp))
+    wide = width // HALVES
 
     def half_copy(c):
-        cols = slice(c * WIDE, (c + 1) * WIDE)
+        cols = slice(c * wide, (c + 1) * wide)
         return pltpu.make_async_copy(half.at[:, cols], half_out.at[:, cols], half_s.at[c])
 
     def half_part(c):
-        tab = slice(c * WIDE, (c + 1) * WIDE)
+        tab = slice(c * wide, (c + 1) * wide)
         half[:, tab] = dot3(mat_h[local, :], mat_l[local, :], tab_h[tab, :], tab_l[tab, :], NT)
         half_copy(c).start()
 
-    produce(0)
-    produce(1)
-    settle(0)
-    start(first[0])
-    produce(2)
-    settle(1)
-    start(first[1])
-    advance(0, 0)
-    produce(3)
-    settle(2)
-    start(first[2])
-    advance(1, 0)
-    advance(0, 1)
+    def steps(q, carry):
+        produce(2 * q, own_z, q)
+
+        @pl.when(q >= 1)
+        def _():
+            settle(2 * q - 1, own_y, q - 1)
+            start(round_y(q - 1))
+
+        produce(2 * q + 1, own_y, q)
+        settle(2 * q, own_z, q)
+        start(round_z(q))
+
+        @pl.when(q >= 1)
+        def _():
+            advance(round_z(q - 1), 0)
+
+        @pl.when(q >= 2)
+        def _():
+            advance(round_y(q - 2), 0)
+            advance(round_z(q - 2), 1)
+
+        @pl.when(q >= 3)
+        def _():
+            advance(round_z(q - 3), 2)
+
+        return carry
+
+    lax.fori_loop(0, some, steps, 0)
+    settle(pieces - 1, own_y, 3)
+    start(round_y(3))
     half_part(0)
-    settle(3)
-    start(first[3])
+    advance(round_y(2), 0)
+    advance(round_z(3), 0)
+    advance(round_z(2), 1)
+    advance(round_z(1), 2)
+    end_y(0)
     half_part(1)
-    advance(0, 2)
-    advance(2, 0)
+    end_z(0)
+    end_y(1)
+    start(chain_z)
+    advance(round_y(3), 0)
+    advance(round_z(3), 1)
+    advance(round_z(2), 2)
+    end_z(1)
+    last_y[0].start()
+    end_y(2)
+    advance(chain_z, 0)
     half_part(2)
-    turn_corner(1)
-    advance(3, 0)
-    advance(2, 1)
+    end_y(3)
+    last_z.start()
+    advance(round_z(3), 2)
+    advance(chain_z, 1)
+    end_z(2)
     half_part(3)
-    turn_corner(0)
-    advance(2, 2)
-    turn_corner(3)
-    turn_corner(2)
-    for p in (1, 0, 3, 2):
-        finish(p)
+    advance(chain_z, 2)
+    end_z(3)
+    last_y[1].start()
+    give(0, 0, last_y[:1])
+    give(1, 0, chain_z)
+    give(1, 1, [last_z])
+    give(0, 1, last_y[1:])
 
     for d in range(1, n_grp):
         tell(d).wait_send()
     for way in range(2):
         for step in range(3):
             pass_on(way, step).wait_send()
-    for group in first + second:
-        for way in group:
+    for way in last_y + [last_z] + chain_z:
+        way.drain()
+    for c in range(HALVES):
+        half_copy(c).wait()
+
+    def drain(i, carry):
+        for way in round_z(i) + round_y(i):
             way.drain()
-    for p in range(pieces):
-        over_core(p).wait_send()
-        half_copy(p).wait()
+        for p in (2 * i, 2 * i + 1):
+            over_core(p).wait_send()
+        return carry
+
+    lax.fori_loop(0, some, drain, 0)
 
 
 def on_device(blocks, block_home, block_group, block_slot, pair_funcs, occ_coef, vir_coef):
@@ -432,20 +507,23 @@
             pltpu.VMEM((width, rows), BF16),
             pltpu.VMEM((rows, rows), BF16),
             pltpu.VMEM((rows, rows), BF16),
+            pltpu.VMEM((width // n_grp, rows), F32),
             pltpu.VMEM((NC, kept, rows), BF16),
             pltpu.VMEM((NC, kept, rows), BF16),
             pltpu.VMEM((pieces, NZ, NY, SUB, WIDE), F32),
             pltpu.VMEM((pieces, NZ, NY, SUB, WIDE), F32),
-            pltpu.VMEM((pieces, NZ, NY, SUB, WIDE), F32),
+            pltpu.VMEM((some, NZ, NY, SUB, WIDE), F32),
+            pltpu.VMEM((some, NZ, NY, SUB, WIDE), F32),
             pltpu.VMEM((rows_dev, width), F32),
             pltpu.VMEM((some, 2, yh, NZ, SUB, WIDE), F32),
             pltpu.VMEM((some, 2, zh, NY, SUB, WIDE), F32),
-            pltpu.VMEM((some, NY, SUB, WIDE), F32),
-            pltpu.VMEM((some, NZ, SUB, WIDE), F32),
+            pltpu.VMEM((some // 2, NY, 2, SUB, WIDE), F32),
+            pltpu.VMEM((NZ, 2, SUB, WIDE), F32),
+            pltpu.VMEM((2, zh, 2, SUB, WIDE), F32),
             dma((n_grp,)), dma((n_grp,)), dma((2, 3)), dma((2, 3)), dma((7,)),
-            dma((pieces,)), dma((pieces,)), dma((pieces,)),
+            dma((pieces,)), dma((pieces,)), dma((HALVES,)),
             dma((some, 2, yh)), dma((some, 2, yh)), dma((some, 2, zh)), dma((some, 2, zh)),
-            dma((some, NY)), dma((some, NY)), dma((some, NZ)), dma((some, NZ)),
+            dma((some // 2, NY)), dma((some // 2, NY)), dma((NZ,)), dma((NZ,)), dma((2, zh)), dma((2, zh)),
         ],
         compiler_params=pltpu.CompilerParams(
             collective_id=0, has_side_effects=True, vmem_limit_bytes=VMEM_MIB * 2**20

time: 65.8 us -> 67.3 us (1.023)
  Pallas kernels: 60.3 us -> 62.2 us
    pallas_call x1, Pallas kernels: 60.3 us -> 62.2 us  [on_device(): pl.pallas_call(functools.partial(column_kernel, n_vir, tiles_dev), out_sh...]
where the time goes in v4:
time: 67.3 us; the launch traced here: 66.7 us
  Pallas kernels  62.2 us (92%)
  local copies, waits for them, and re-layouts  3.8 us (6%)
    pallas_call x1, Pallas kernels, on_device(): pl.pallas_call(functools.partial(column_kernel, n_vir, tiles_dev), out_sh...  62.2 us
    unnamed x4, local copies, waits for them, and re-layouts  3.8 us

profile of v4, /device:TPU:8, one launch (start us, length us, event | category | flops | bytes accessed | tf_op | source)
XLA Modules:
  0.0 66.7 jit_solution(6211408299144873576)
XLA Ops:
  0.6 62.2 %shard_map.86 = (f32[256,2048]{1,0:T(8,128)}, f32[8,2048]{1,0:T(8,128)}) custom-call(s32[4]{0:T(128)} %home_in.1, s32[4]{0:T(128)} %bitcast.3, s32[4]{0:T(128)} %slot_in.1, s32[2,256]{1,0:T(2,128)} %funcs_in.1, f32[16,1536]{1,0:T(8,128)} %bitcast.2, f32[1536,128]{1,0:T(8,128)} %vir_in.1, f32[4,128,128]{2,1,0:T(8,128)} %blocks_ref.1), custom_call_target="tpu_custom_call" | custom-call | tf_op jit(solution)/shard_map/pallas_call | solution.py:490
  62.8 0.0 copy-start
  62.9 3.2 %copy.11 = f32[256,2048]{1,0:T(8,128)} copy(f32[256,2048]{1,0:T(8,128)} %get-tuple-element.4) | data formatting | bytes 4194304
  66.0 0.0 copy-done
  66.0 0.6 copy.12
Async XLA Ops:
  62.8 3.2 %copy-start = (f32[8,2048]{1,0:T(8,128)S(1)}, f32[8,2048]{1,0:T(8,128)}, u32[]{:S(2)}) copy-start(f32[8,2048]{1,0:T(8,128)} %get-tuple-element.5) | copy-start | bytes 196612

commit v5 on v3

--- a/solution.py
+++ b/solution.py
@@ -168,9 +168,9 @@
 
 def column_kernel(n_vir, tiles_dev, home_in, group_in, slot_in, funcs_in, occ_in, vir_in, blocks_ref,
                   half_out, orb_out, home_ref, group_ref, slot_ref, funcs_ref, occ_ref, vir_ref, infos, every, flip, coef_ref, tab_h, tab_l, mat_h, mat_l, g_h, g_l,
-                  away, near, own, half, y1, z1, y2, z2,
+                  away, near, own, half, y1, z1, y2, z2, zc,
                   info_s, info_r, block_s, block_r, own_s, core_s, core_r, half_s,
-                  y1_s, y1_r, z1_s, z1_r, y2_s, y2_r, z2_s, z2_r):
+                  y1_s, y1_r, z1_s, z1_r, y2_s, y2_r, z2_s, z2_r, zc_s, zc_r):
     n_grp, per_dev, tile, _ = every.shape
     n_occ = occ_ref.shape[0]
     width, rows = tab_h.shape
@@ -316,7 +316,12 @@
             second.append([Direct(y, NY, lambda v, p=p: own.at[p, z, v], y2.at[i], y2_s.at[i], y2_r.at[i], to_y)])
         else:
             first.append(chains(p, NY, y, lambda v, p=p: own.at[p, :, v], y1.at[i], y1_s.at[i], y1_r.at[i], to_y))
-            second.append([Direct(z, NZ, lambda v, p=p: own.at[p, v, y], z2.at[i], z2_s.at[i], z2_r.at[i], to_z)])
+            if i == 0:
+                hops = lengths(NZ)[0]
+                second.append([Chain(z, NZ, (1, -1)[d], hops[d], lambda v, p=p: own.at[p, v, y], zc.at[d], zc_s.at[d],
+                                     zc_r.at[d], to_z) for d in range(2)])
+            else:
+                second.append([Direct(z, NZ, lambda v, p=p: own.at[p, v, y], z2, z2_s, z2_r, to_z)])
 
     def start(group):
         for way in group:
@@ -333,6 +338,10 @@
             total = way.arrive(total)
         here[...] = total
         start(second[p])
+
+    def go_on(j):
+        for way in second[1]:
+            way.advance(j)
 
     def finish(p):
         total = own[p, z, y]
@@ -376,10 +385,13 @@
     advance(2, 1)
     half_part(3)
     turn_corner(0)
+    go_on(0)
     advance(2, 2)
     turn_corner(3)
+    go_on(1)
     turn_corner(2)
-    for p in (1, 0, 3, 2):
+    go_on(2)
+    for p in (0, 1, 3, 2):
         finish(p)
 
     for d in range(1, n_grp):
@@ -441,11 +453,12 @@
             pltpu.VMEM((some, 2, yh, NZ, SUB, WIDE), F32),
             pltpu.VMEM((some, 2, zh, NY, SUB, WIDE), F32),
             pltpu.VMEM((some, NY, SUB, WIDE), F32),
-            pltpu.VMEM((some, NZ, SUB, WIDE), F32),
+            pltpu.VMEM((NZ, SUB, WIDE), F32),
+            pltpu.VMEM((2, zh, SUB, WIDE), F32),
             dma((n_grp,)), dma((n_grp,)), dma((2, 3)), dma((2, 3)), dma((7,)),
             dma((pieces,)), dma((pieces,)), dma((pieces,)),
             dma((some, 2, yh)), dma((some, 2, yh)), dma((some, 2, zh)), dma((some, 2, zh)),
-            dma((some, NY)), dma((some, NY)), dma((some, NZ)), dma((some, NZ)),
+            dma((some, NY)), dma((some, NY)), dma((NZ,)), dma((NZ,)), dma((2, zh)), dma((2, zh)),
         ],
         compiler_params=pltpu.CompilerParams(
             collective_id=0, has_side_effects=True, vmem_limit_bytes=VMEM_MIB * 2**20

time: 65.8 us -> 64.5 us (0.980); the launches traced: 64.8 us -> 64.4 us
  no operation moved by 1% of the time
where the time goes in v5:
time: 64.5 us; the launch traced here: 64.4 us
  Pallas kernels  59.9 us (93%)
  local copies, waits for them, and re-layouts  3.8 us (6%)
  between operations  0.65 us (1%)
    pallas_call x1, Pallas kernels, on_device(): pl.pallas_call(functools.partial(column_kernel, n_vir, tiles_dev), out_sh...  59.9 us
    unnamed x4, local copies, waits for them, and re-layouts  3.8 us

profile of v5, /device:TPU:8, one launch (start us, length us, event | category | flops | bytes accessed | tf_op | source)
XLA Modules:
  0.0 64.4 jit_solution(16884783283255964601)
XLA Ops:
  0.6 59.9 %shard_map.86 = (f32[256,2048]{1,0:T(8,128)}, f32[8,2048]{1,0:T(8,128)}) custom-call(s32[4]{0:T(128)} %home_in.1, s32[4]{0:T(128)} %bitcast.3, s32[4]{0:T(128)} %slot_in.1, s32[2,256]{1,0:T(2,128)} %funcs_in.1, f32[16,1536]{1,0:T(8,128)} %bitcast.2, f32[1536,128]{1,0:T(8,128)} %vir_in.1, f32[4,128,128]{2,1,0:T(8,128)} %blocks_ref.1), custom_call_target="tpu_custom_call" | custom-call | tf_op jit(solution)/shard_map/pallas_call | solution.py:427
  60.6 0.0 copy-start
  60.6 3.2 %copy.11 = f32[256,2048]{1,0:T(8,128)} copy(f32[256,2048]{1,0:T(8,128)} %get-tuple-element.4) | data formatting | bytes 4194304
  63.7 0.0 copy-done
  63.7 0.6 copy.12
Async XLA Ops:
  60.6 3.2 %copy-start = (f32[8,2048]{1,0:T(8,128)S(1)}, f32[8,2048]{1,0:T(8,128)}, u32[]{:S(2)}) copy-start(f32[8,2048]{1,0:T(8,128)} %get-tuple-element.5) | copy-start | bytes 196612

commit v6 on v5

--- a/solution.py
+++ b/solution.py
@@ -110,26 +110,33 @@
         tab_l[i * n_vir : (i + 1) * n_vir, cols] = low
 
 
-def build_matrix(info_ref, every, flip, mat_h, mat_l, tiles_dev):
+def build_matrix(info_ref, every, mat_h, mat_l, tiles_dev):
     n_grp, per_dev, tile, _ = every.shape
     n_tiles = n_grp * tiles_dev
-    def body(step, carry):
-        h, t = lax.div(step, n_tiles), lax.rem(step, n_tiles)
-        dev_h, dev_t = lax.div(h, tiles_dev), lax.div(t, tiles_dev)
+
+    def direct(h, t):
+        dev = lax.div(h, tiles_dev)
         total = jnp.zeros((tile, tile), F32)
         for j in range(per_dev):
-            code = info_ref[dev_h, j : j + 1, :]
+            code = info_ref[dev, j : j + 1, :]
             here = jnp.logical_and(code[:, :tile] == h, code[:, tile:] == t)
-            total = total + jnp.where(here, every[dev_h, j], 0.0)
-            code = info_ref[dev_t, j : j + 1, :]
-            here = jnp.logical_and(code[:, :tile] == t, code[:, tile:] == h)
-            total = total + jnp.where(here, flip[dev_t, j], 0.0)
-        high, low = split(total)
+            total = total + jnp.where(here, every[dev, j], 0.0)
+        return total
+
+    def store(value, h, t):
+        high, low = split(value)
         mat_h[chunk(h, tile), chunk(t, tile)] = high
         mat_l[chunk(h, tile), chunk(t, tile)] = low
+
+    def body(step, carry):
+        h = lax.rem(step, n_tiles)
+        t = lax.rem(h + lax.div(step, n_tiles), n_tiles)
+        value = direct(h, t) + direct(t, h).T
+        store(value, h, t)
+        store(value.T, t, h)
         return carry
 
-    lax.fori_loop(0, n_tiles * n_tiles, body, 0)
+    lax.fori_loop(0, n_tiles * (n_tiles + 1) // 2, body, 0)
 
 
 class Direct:
@@ -167,7 +174,7 @@
 
 
 def column_kernel(n_vir, tiles_dev, home_in, group_in, slot_in, funcs_in, occ_in, vir_in, blocks_ref,
-                  half_out, orb_out, home_ref, group_ref, slot_ref, funcs_ref, occ_ref, vir_ref, infos, every, flip, coef_ref, tab_h, tab_l, mat_h, mat_l, g_h, g_l,
+                  half_out, orb_out, home_ref, group_ref, slot_ref, funcs_ref, occ_ref, vir_ref, infos, every, coef_ref, tab_h, tab_l, mat_h, mat_l, g_h, g_l,
                   away, near, own, half, y1, z1, y2, z2, zc,
                   info_s, info_r, block_s, block_r, own_s, core_s, core_r, half_s,
                   y1_s, y1_r, z1_s, z1_r, y2_s, y2_r, z2_s, z2_r, zc_s, zc_r):
@@ -180,7 +187,6 @@
     y = lax.rem(lax.div(pair, NC), NY)
     z = lax.div(pair, NC * NY)
     right, left = ring(grp + 1, n_grp), ring(grp - 1, n_grp)
-    far = ring(grp + 2, n_grp)
 
     def at(z_, y_, core_):
         return (grp, (z_ * NY + y_) * NC + core_)
@@ -259,19 +265,11 @@
         pass_on(way, 0).wait_recv()
         pass_on(way, 2).start()
 
-    def turn(g, which):
-        for j in range(which.start, which.stop):
-            flip[g, j] = every[g, j].T
-
     mine_copy.wait()
-    turn(grp, slice(0, per_dev))
-    for way in range(2):
-        pass_on(way, 1).wait_recv()
-        turn((left, right)[way], slice(0, per_dev))
-    for way in range(2):
-        pass_on(way, 2).wait_recv()
-        turn(far, parts_of[way])
-    build_matrix(infos, every, flip, mat_h, mat_l, tiles_dev)
+    for step in (1, 2):
+        for way in range(2):
+            pass_on(way, step).wait_recv()
+    build_matrix(infos, every, mat_h, mat_l, tiles_dev)
     share = chunk(grp, mine)
 
     def make_g(c, carry):
@@ -438,7 +436,6 @@
             pltpu.VMEM((nb, n_vir), F32),
             pltpu.VMEM((n_grp, INFO, rows_dev), I32),
             pltpu.VMEM((n_grp, per_dev, tile, tile), F32),
-            pltpu.VMEM((n_grp, per_dev, tile, tile), F32),
             pltpu.VMEM((2 * (n_occ + n_vir), nb), BF16),
             pltpu.VMEM((width, rows), BF16),
             pltpu.VMEM((width, rows), BF16),

time: 64.5 us -> 67 us (1.039)
  Pallas kernels: 59.9 us -> 62.4 us
    pallas_call x1, Pallas kernels: 59.9 us -> 62.4 us  [on_device(): pl.pallas_call(functools.partial(column_kernel, n_vir, tiles_dev), out_sh...]
where the time goes in v6:
time: 67 us; the launch traced here: 66.8 us
  Pallas kernels  62.4 us (93%)
  local copies, waits for them, and re-layouts  3.8 us (6%)
    pallas_call x1, Pallas kernels, on_device(): pl.pallas_call(functools.partial(column_kernel, n_vir, tiles_dev), out_sh...  62.4 us
    unnamed x4, local copies, waits for them, and re-layouts  3.8 us

profile of v6, /device:TPU:8, one launch (start us, length us, event | category | flops | bytes accessed | tf_op | source)
XLA Modules:
  0.0 66.8 jit_solution(5931119689738539101)
XLA Ops:
  0.6 62.4 %shard_map.86 = (f32[256,2048]{1,0:T(8,128)}, f32[8,2048]{1,0:T(8,128)}) custom-call(s32[4]{0:T(128)} %home_in.1, s32[4]{0:T(128)} %bitcast.3, s32[4]{0:T(128)} %slot_in.1, s32[2,256]{1,0:T(2,128)} %funcs_in.1, f32[16,1536]{1,0:T(8,128)} %bitcast.2, f32[1536,128]{1,0:T(8,128)} %vir_in.1, f32[4,128,128]{2,1,0:T(8,128)} %blocks_ref.1), custom_call_target="tpu_custom_call" | custom-call | tf_op jit(solution)/shard_map/pallas_call | solution.py:425
  63.0 0.0 copy-start
  63.0 3.2 %copy.11 = f32[256,2048]{1,0:T(8,128)} copy(f32[256,2048]{1,0:T(8,128)} %get-tuple-element.4) | data formatting | bytes 4194304
  66.2 0.0 copy-done
  66.2 0.6 copy.12
Async XLA Ops:
  63.0 3.2 %copy-start = (f32[8,2048]{1,0:T(8,128)S(1)}, f32[8,2048]{1,0:T(8,128)}, u32[]{:S(2)}) copy-start(f32[8,2048]{1,0:T(8,128)} %get-tuple-element.5) | copy-start | bytes 196612
